TPU v7x, 512 devices: a whole 4x8x8 slice. The times are simulated.
512 devices in a mesh: dp: 8 (over x, z_lo), seq: 8 (over z_hi, core), head: 8 (over y).
Axes of the slice: x: 4, y: 8, z: 8 (z_hi: 4, z_lo: 2; z = z_hi * 2 + z_lo), core: 2. Of those that a mesh axis runs over, the one named last changes fastest.
Arguments:
- patch_in: bfloat16 [8, 1024, 1536], P('dp', 'head', 'seq'), may hold values from -6 to 6
- enc_weight: bfloat16 [1536, 1536], P('seq'), may hold values from -0.15625 to 0.15625
- enc_gain: float32 [1536], replicated, may hold values from 0.1 to 1.9
- enc_bias: float32 [1536], replicated, may hold values from -3 to 3
- interp_index: int32 [8, 2304], P('dp', 'seq'), may hold values from 0 to 1023, as said below
- queries: bfloat16 [8, 2304, 3072], P('dp', 'seq', 'head'), may hold values from -64 to 64
- key_rows: bfloat16 [8, 2304, 3072], P('dp', 'seq', 'head'), may hold values from -64 to 64
- value_rows: bfloat16 [8, 2304, 3072], P('dp', 'seq', 'head'), may hold values from -6 to 6
- proj_weight: bfloat16 [1536, 3072], P(None, 'head'), may hold values from -0.109375 to 0.109375
Outputs:
- attn_out: bfloat16 [8, 2304, 3072], P('dp', 'seq', 'head')
- cosine: float32 [8, 2304], P('dp', 'seq')
- grad_attn: bfloat16 [8, 2304, 3072], P('dp', 'seq', 'head')
- grad_proj: float32 [1536, 3072], P(('dp', 'seq'), 'head')
Inputs may be any that keep to these rules, and one draw needn't show every extreme that they name: interp_index[b, t] names a patch of the same sample's crop.
All inputs are finite; a program needn't handle non-finite values.
Results may differ from a plain program's by a relative error of at most 0.017.
Values may be sent and summed in bfloat16 or wider, within the bound.
A program may use at most 64 MiB of HBM per device.

v0:
```python
import jax
import jax.numpy as jnp
from jax import lax
from jax.sharding import PartitionSpec as P

HD = 128


layer_eps = 1e-06
cos_eps = 1e-06


def normalize(encoded, enc_gain, enc_bias):
    average = jnp.mean(encoded, axis=-1, keepdims=True)
    centred = encoded - average
    variance = jnp.mean(centred * centred, axis=-1, keepdims=True)
    return (centred * lax.rsqrt(variance + layer_eps) * enc_gain + enc_bias).astype(jnp.bfloat16)


def pick_rows(row_of_token, portion):
    inside = (row_of_token >= 0) & (row_of_token < portion.shape[0])
    taken = jnp.take(portion, jnp.clip(row_of_token, 0, portion.shape[0] - 1), axis=0)
    return jnp.where(inside[:, None], taken.astype(jnp.float32), 0.0)


def on_device(
    patch_in,
    enc_weight,
    enc_gain,
    enc_bias,
    interp_index,
    queries,
    key_rows,
    value_rows,
    proj_weight,
):
    local_patches = patch_in[0]
    tok_index = interp_index[0]
    n_seq = lax.axis_size("seq")
    n_head = lax.axis_size("head")
    share = lax.psum_scatter(
        jnp.dot(local_patches, enc_weight, preferred_element_type=jnp.float32),
        "seq",
        scatter_dimension=0,
        tiled=True,
    )
    targets = normalize(share, enc_gain, enc_bias)
    per_device = targets.shape[0]
    head_block = per_device * n_seq
    owner = tok_index % head_block // per_device * n_head + tok_index // head_block
    gathered_row = owner * per_device + tok_index % per_device
    aligned = pick_rows(gathered_row, lax.all_gather(targets, ("seq", "head"), axis=0, tiled=True))
    local_queries = queries[0]
    key_all, value_all = (
        lax.all_gather(key_rows[0], "seq", axis=0, tiled=True),
        lax.all_gather(value_rows[0], "seq", axis=0, tiled=True),
    )
    score_scale = HD ** (-0.5)
    head_outs = []
    for head_idx in range(local_queries.shape[1] // HD):
        lower = head_idx * HD
        q_head = local_queries[:, lower : lower + HD]
        k_head = key_all[:, lower : lower + HD]
        v_head = value_all[:, lower : lower + HD]
        scores = (
            lax.dot_general(
                q_head, k_head, (((1,), (1,)), ((), ())), preferred_element_type=jnp.float32
            )
            * score_scale
        )
        row_max = jnp.max(scores, axis=1, keepdims=True)
        exponent = jnp.exp(scores - row_max)
        probs = (exponent / jnp.sum(exponent, axis=1, keepdims=True)).astype(jnp.bfloat16)
        head_outs.append(jnp.dot(probs, v_head, preferred_element_type=jnp.float32))
    attn = jnp.concatenate(head_outs, axis=1).astype(jnp.bfloat16)
    partial_proj = lax.dot_general(
        attn, proj_weight, (((1,), (1,)), ((), ())), preferred_element_type=jnp.float32
    )
    projected = lax.psum(partial_proj.astype(jnp.bfloat16), "head").astype(jnp.float32)
    proj_norm = jnp.sqrt(jnp.sum(projected * projected, axis=1) + cos_eps)
    aligned_norm = jnp.sqrt(jnp.sum(aligned * aligned, axis=1) + cos_eps)
    cosine = jnp.sum(projected * aligned, axis=1) / (proj_norm * aligned_norm)
    grad_projected = (
        -(
            aligned / (proj_norm * aligned_norm)[:, None]
            - (cosine / (proj_norm * proj_norm))[:, None] * projected
        )
    ).astype(jnp.bfloat16)
    grad_attn = jnp.dot(grad_projected, proj_weight, preferred_element_type=jnp.float32).astype(
        jnp.bfloat16
    )
    grad_proj = lax.psum_scatter(
        lax.dot_general(
            grad_projected, attn, (((0,), (0,)), ((), ())), preferred_element_type=jnp.float32
        ),
        ("dp", "seq"),
        scatter_dimension=0,
        tiled=True,
    )
    return (attn[None], cosine[None], grad_attn[None], grad_proj)


def solution(mesh):
    placed = (
        P("dp", "head", "seq"),
        P("seq", None),
        P(),
        P(),
        P("dp", "seq"),
        P("dp", "seq", "head"),
        P("dp", "seq", "head"),
        P("dp", "seq", "head"),
        P(None, "head"),
    )
    return jax.shard_map(
        on_device,
        mesh=mesh,
        in_specs=placed,
        out_specs=(
            P("dp", "seq", "head"),
            P("dp", "seq"),
            P("dp", "seq", "head"),
            P(("dp", "seq"), "head"),
        ),
        check_vma=False,
    )
```

profile of v0, /device:TPU:1, one launch (start us, length us, event | category | flops | bytes accessed | tf_op | source)
XLA Modules:
  0.0 572.9 jit_solution(17670895811050727808)
XLA Ops:
  7.2 0.0 copy-start
  7.2 0.0 copy-start.9
  7.2 0.0 copy-start.8
  7.2 0.0 copy-start.7
  7.2 0.0 reduce-scatter.6.cloned.1.call-start
  7.3 2.4 fusion.25
  9.6 0.0 reduce-scatter.6.cloned.1.call-update
  9.6 0.0 all-gather.8.cloned.1.call-start
  9.7 0.7 all-gather.8.cloned.1.call-update
  10.4 0.0 all-gather.10.cloned.1.call-start
  10.4 0.7 all-gather.10.cloned.1.call-update
  11.1 0.0 all-gather.6.cloned.1.call-start
  11.2 45.2 %reduce-scatter.6.cloned.1.call-done = f32[16,1536]{1,0:T(8,128)} async-done(((f32[128,1536]{1,0:T(8,128)}), f32[16,1536]{1,0:T(8,128)}) %reduce-scatter.6.cloned.1.call-update) | async-done | bytes 98320 | tf_op jit(solution)/shard_map/reduce_scatter | solution.py:41
  56.4 1.0 reduce_sum.75
  57.4 1.1 multiply_reduce_fusion.1
  58.5 0.0 copy-done.9
  58.5 0.0 copy-done.8
  58.5 1.6 add_convert_fusion
  60.1 0.0 all-gather.6.cloned.1.call-update
  60.1 0.0 all-reduce.3.cloned.1.call-start
  60.2 36.0 %all-gather.8.cloned.1.call-done = bf16[1,2304,384]{2,1,0:T(8,128)(2,1)} async-done(((bf16[1,288,384]{2,1,0:T(8,128)(2,1)}), bf16[1,2304,384]{2,1,0:T(8,128)(2,1)}) %all-gather.8.cloned.1.call-update) | async-done | bytes 1769488 | tf_op jit(solution)/shard_map/all_gather | solution.py:55
  96.2 0.0 copy-done.7
  96.2 0.0 copy-start.6
  96.2 1.8 fusion.42
  98.0 0.0 copy-start.1
  98.0 0.5 fusion
  98.5 0.0 copy-done.6
  98.5 0.6 fusion.41
  99.1 0.4 copy-done.1
  99.5 0.0 copy-start.2
  99.5 0.5 fusion.1
  100.0 0.6 fusion.40
  100.6 0.4 copy-done.2
  101.1 0.0 copy-start.4
  101.1 1.6 copy-done.4
  102.6 0.5 fusion.2
  103.1 30.5 %all-gather.10.cloned.1.call-done = bf16[1,2304,384]{2,1,0:T(8,128)(2,1)} async-done(((bf16[1,288,384]{2,1,0:T(8,128)(2,1)}), bf16[1,2304,384]{2,1,0:T(8,128)(2,1)}) %all-gather.10.cloned.1.call-update) | async-done | bytes 1769488 | tf_op jit(solution)/shard_map/all_gather | solution.py:56
  133.6 0.0 copy-start.3
  133.6 0.0 copy-start.11
  133.6 2.6 fusion.14
  136.2 0.1 copy-done.3
  136.3 0.5 copy-done.11
  136.9 0.0 copy-start.5
  136.9 0.6 fusion.13
  137.5 1.1 copy-done.5
  138.6 0.6 fusion.12
  139.2 0.0 copy-done
  139.2 0.0 copy-start.10
  139.2 1.6 convolution_convert_fusion
  140.8 0.0 all-reduce.3.cloned.1.call-update
  140.9 0.0 reduce-scatter.8.cloned.1.call-start
  140.9 0.0 copy-done.10
  141.0 80.0 %all-gather.6.cloned.1.call-done = bf16[1024,1536]{1,0:T(8,128)(2,1)} async-done(((bf16[16,1536]{1,0:T(8,128)(2,1)}), bf16[1024,1536]{1,0:T(8,128)(2,1)}) %all-gather.6.cloned.1.call-update) | async-done | bytes 3145744 | tf_op jit(solution)/shard_map/all_gather | solution.py:52
  221.1 6.0 %gather_fusion = bf16[288,1536]{1,0:T(8,128)(2,1)S(1)} fusion(bf16[1024,1536]{1,0:T(8,128)(2,1)} %all-gather.6.cloned.1.call-done, s32[1024]{0:T(1024)S(1)} %pad_clamp_fusion), kind=kCustom, calls=%fused_computation | custom fusion | bytes 1770624 | tf_op jit(solution)/shard_map/jit(_take)/gather | solution.py:22
  227.0 68.5 %all-reduce.3.cloned.1.call-done = bf16[288,1536]{1,0:T(8,128)(2,1)} async-done(((bf16[288,1536]{1,0:T(8,128)(2,1)}), bf16[288,1536]{1,0:T(8,128)(2,1)}) %all-reduce.3.cloned.1.call-update) | async-done | bytes 884752 | tf_op jit(solution)/shard_map/psum | solution.py:79
  295.5 2.0 multiply_reduce_fusion
  297.5 1.8 fusion.7
  299.3 2.3 fusion.21
  301.6 0.0 reduce-scatter.8.cloned.1.call-update
  301.6 0.7 pad_maximum_fusion
  302.4 0.6 div.121
  302.9 1.3 fusion.11
  304.2 261.8 %reduce-scatter.8.cloned.1.call-done = f32[24,384]{1,0:T(8,128)} async-done(((f32[1536,384]{1,0:T(8,128)}), f32[24,384]{1,0:T(8,128)}) %reduce-scatter.8.cloned.1.call-update) | async-done | bytes 36880
  (9 shorter events, 0.1 us)
Async XLA Ops:
  7.2 132.1 %copy-start = (bf16[1536,384]{1,0:T(8,128)(2,1)S(1)}, bf16[1536,384]{1,0:T(8,128)(2,1)}, u32[]{:S(2)}) copy-start(bf16[1536,384]{1,0:T(8,128)(2,1)} %param.17) | copy-start | bytes 3538948
  7.2 51.3 %copy-start.9 = (f32[1536]{0:T(1024)S(1)}, f32[1536]{0:T(1024)}, u32[]{:S(2)}) copy-start(f32[1536]{0:T(1024)} %param.11) | copy-start | bytes 18436
  7.2 51.3 %copy-start.8 = (f32[1536]{0:T(1024)S(1)}, f32[1536]{0:T(1024)}, u32[]{:S(2)}) copy-start(f32[1536]{0:T(1024)} %param.12) | copy-start | bytes 18436
  7.2 89.0 %copy-start.7 = (bf16[1,288,384]{2,1,0:T(8,128)(2,1)S(1)}, bf16[1,288,384]{2,1,0:T(8,128)(2,1)}, u32[]{:S(2)}) copy-start(bf16[1,288,384]{2,1,0:T(8,128)(2,1)} %param.14) | copy-start | bytes 663556
  7.2 49.1 %reduce-scatter.6.cloned.1.call-start = ((), (), s32[]{:S(2)}) async-start(), calls=%async_computation.3 | async-start | bytes 884736 | tf_op jit(solution)/shard_map/reduce_scatter | solution.py:41
  9.6 86.5 %all-gather.8.cloned.1.call-start = ((), (), s32[]{:S(2)}) async-start(), calls=%async_computation.5 | async-start | bytes 1990656 | tf_op jit(solution)/shard_map/all_gather | solution.py:55
  10.4 123.2 %all-gather.10.cloned.1.call-start = ((), (), s32[]{:S(2)}) async-start(), calls=%async_computation.6 | async-start | bytes 1990656 | tf_op jit(solution)/shard_map/all_gather | solution.py:56
  11.1 209.9 %all-gather.6.cloned.1.call-start = ((), (), s32[]{:S(2)}) async-start(), calls=%async_computation.4 | async-start | bytes 3194880 | tf_op jit(solution)/shard_map/all_gather | solution.py:52
  60.1 235.4 %all-reduce.3.cloned.1.call-start = ((), (), s32[]{:S(2)}) async-start(), calls=%async_computation.2 | async-start | bytes 1769472 | tf_op jit(solution)/shard_map/psum | solution.py:79
  96.2 2.3 copy-start.6
  98.0 1.5 copy-start.1
  99.5 1.6 copy-start.2
  101.1 1.6 copy-start.4
  133.6 2.7 copy-start.3
  133.6 3.2 copy-start.11
  136.9 1.7 copy-start.5
  139.2 1.7 copy-start.10
  140.9 425.2 %reduce-scatter.8.cloned.1.call-start = ((), (), s32[]{:S(2)}) async-start(), calls=%async_computation.7 | async-start | bytes 2396160
Sparse Core Ops, SparseCore 0:
  10.9 45.4 reduce-scatter.5
  58.7 37.4 all-gather.7
  98.5 35.0 all-gather.9
  137.8 83.1 all-gather.5
  223.4 72.0 all-reduce.2
  301.8 264.2 reduce-scatter.7
where the time goes:
time: 577 us; the launch traced here: 573 us
  waiting for transfers between devices  523 us (91%)
  matrix products  14.5 us (3%)
  between operations  14.3 us (2%)
  local copies, waits for them, and re-layouts  10.7 us (2%)
  other arithmetic  9.87 us (2%)
    unnamed x7, waiting for transfers between devices  263 us
    all_gather x1, waiting for transfers between devices, on_device(): lax.all_gather(targets, ('seq', 'head'), axis=0, tiled=True)  80 us
    psum x1, waiting for transfers between devices, on_device(): lax.psum(partial_proj.astype(jnp.bfloat16), 'head').astype(jnp.float32)  68.5 us
    reduce_scatter x1, waiting for transfers between devices, on_device(): lax.psum_scatter(jnp.dot(local_patches, enc_weight, preferred_element_typ...  45.2 us
    all_gather x1, waiting for transfers between devices, on_device(): lax.all_gather(key_rows[0], 'seq', axis=0, tiled=True)  36 us
    all_gather x1, waiting for transfers between devices, on_device(): lax.all_gather(value_rows[0], 'seq', axis=0, tiled=True)  30.5 us
  transfers between devices with their start and end apart: 6, of which 6 were waited for; matrix products, arithmetic and copies ran while one was open for 4% of the time, Pallas kernels for 0%

commit v1 on v0

v1 whole, which is shorter than its diff:
```python
import jax
import jax.numpy as jnp
from jax import lax
from jax.experimental import pallas as pl
from jax.experimental.pallas import tpu as pltpu
from jax.sharding import PartitionSpec as P

MESH = pl.DeviceIdType.MESH
BF = jnp.bfloat16
F32 = jnp.float32

E = 1536
HD = 128
NH = 3
DA = NH * HD
TOK = 288
HALF = 144
SUB = 48
PHASES = 3
EC = 384

layer_eps = 1e-06
cos_eps = 1e-06


def remote(src, dst, send, recv, where):
    return pltpu.make_async_remote_copy(
        src_ref=src, dst_ref=dst, send_sem=send, recv_sem=recv, device_id=where, device_id_type=MESH
    )


def greet(peers):
    barrier = pltpu.get_barrier_semaphore()
    for peer in peers:
        pl.semaphore_signal(barrier, inc=1, device_id=peer, device_id_type=MESH)
    pl.semaphore_wait(barrier, len(peers))


def places():
    dp, seq, y = lax.axis_index("dp"), lax.axis_index("seq"), lax.axis_index("head")
    return dp // 2, dp % 2, seq // 2, seq % 2, y


def front(
    patch, enc_w, gain, bias, idx, q, k, v, attn, aligned,
    kbuf, vbuf, part, e1r, e2s, e2r, e3s, e3r, tgt, table,
    k_s, k_r, v_s, v_r, e_s, e_r, t_s, t_r, g_s, g_r,
):
    x, zl, zh, c, y = places()
    seq = zh * 2 + c
    up, dn, op = (zh + 1) % 4, (zh + 3) % 4, (zh + 2) % 4
    at_up, at_dn, at_sib = {"seq": up * 2 + c}, {"seq": dn * 2 + c}, {"seq": zh * 2 + 1 - c}
    s_up, s_dn, s_op = up * 2 + c, dn * 2 + c, op * 2 + c
    o = 1 - c
    sent = []

    def go(copy):
        copy.start()
        sent.append(copy)

    greet([at_up, at_dn, at_sib] + [{"head": (y + d) % 8} for d in range(1, 8)])

    def own(h):
        cols = slice(h * HD, (h + 1) * HD)
        for n, (src, buf, ss, rs) in enumerate(((k, kbuf, k_s, k_r), (v, vbuf, v_s, v_r))):
            for w, where in enumerate((at_up, at_dn, at_sib)):
                go(remote(src.at[:, cols], buf.at[h, seq], ss.at[h, w], rs.at[h, seq], where))
            buf[h, seq] = src[:, cols]

    def landed(buf, rs, h, s):
        remote(buf.at[h, s], buf.at[h, s], rs.at[h, s], rs.at[h, s], at_sib).wait_recv()

    def forward(buf, ss, rs, h, s, w, where):
        go(remote(buf.at[h, s], buf.at[h, s], ss.at[h, w], rs.at[h, s], where))

    def relay(h):
        landed(kbuf, k_r, h, s_dn)
        forward(kbuf, k_s, k_r, h, s_dn, 3, at_up)
        forward(kbuf, k_s, k_r, h, s_dn, 4, at_sib)
        landed(vbuf, v_r, h, s_up)
        forward(vbuf, v_s, v_r, h, s_up, 3, at_dn)
        forward(vbuf, v_s, v_r, h, s_up, 4, at_sib)
        landed(vbuf, v_r, h, s_dn)
        forward(vbuf, v_s, v_r, h, s_dn, 5, at_sib)
        landed(kbuf, k_r, h, s_up)
        forward(kbuf, k_s, k_r, h, s_up, 5, at_sib)

    def finish(h):
        landed(kbuf, k_r, h, s_op)
        forward(kbuf, k_s, k_r, h, s_op, 6, at_sib)
        landed(vbuf, v_r, h, s_op)
        forward(vbuf, v_s, v_r, h, s_op, 6, at_sib)

    def attend(h):
        for z in range(4):
            landed(kbuf, k_r, h, z * 2 + o)
        for z in range(4):
            landed(vbuf, v_r, h, z * 2 + o)
        keys = kbuf.at[h]
        values = vbuf.at[h]

        @pl.loop(0, 3)
        def _(b):
            rows = pl.ds(pl.multiple_of(b * 96, 96), 96)
            kk = keys[...].reshape(8 * TOK, HD)
            vv = values[...].reshape(8 * TOK, HD)
            scores = lax.dot_general(
                q[rows, h * HD : (h + 1) * HD], kk, (((1,), (1,)), ((), ())),
                preferred_element_type=F32,
            )
            top = jnp.max(scores, axis=1, keepdims=True)
            expo = jnp.exp((scores - top) * (HD**-0.5))
            total = jnp.sum(expo, axis=1, keepdims=True)
            out = jnp.dot(expo.astype(BF), vv, preferred_element_type=F32)
            attn[rows, h * HD : (h + 1) * HD] = (out / total).astype(BF)

    own(0)
    share = jnp.dot(patch[...], enc_w[...], preferred_element_type=F32)
    for z in range(4):
        for cc in range(2):
            part[z, cc] = share[(2 * z + cc) * 16 : (2 * z + cc + 1) * 16]
    for z in range(4):
        go(remote(part.at[z, o], e1r.at[z], e_s.at[z], e_r.at[z], at_sib))
    for z in range(4):
        remote(part.at[z, o], e1r.at[z], e_s.at[z], e_r.at[z], at_sib).wait_recv()
    far = part[op, c] + e1r[op]
    e2s[0] = far[:, : E // 2].astype(BF)
    e2s[1] = far[:, E // 2 :].astype(BF)
    go(remote(e2s.at[0], e2r.at[0], e_s.at[4], e_r.at[4], at_up))
    go(remote(e2s.at[1], e2r.at[1], e_s.at[5], e_r.at[5], at_dn))
    own(1)
    remote(e2s.at[0], e2r.at[0], e_s.at[4], e_r.at[4], at_up).wait_recv()
    remote(e2s.at[1], e2r.at[1], e_s.at[5], e_r.at[5], at_dn).wait_recv()
    near = part[up, c] + e1r[up]
    e3s[0, :, : E // 2] = (near[:, : E // 2] + e2r[0].astype(F32)).astype(BF)
    e3s[0, :, E // 2 :] = near[:, E // 2 :].astype(BF)
    near = part[dn, c] + e1r[dn]
    e3s[1, :, : E // 2] = near[:, : E // 2].astype(BF)
    e3s[1, :, E // 2 :] = (near[:, E // 2 :] + e2r[1].astype(F32)).astype(BF)
    go(remote(e3s.at[0], e3r.at[0], e_s.at[6], e_r.at[6], at_up))
    go(remote(e3s.at[1], e3r.at[1], e_s.at[7], e_r.at[7], at_dn))
    relay(0)
    own(2)
    remote(e3s.at[0], e3r.at[0], e_s.at[6], e_r.at[6], at_up).wait_recv()
    remote(e3s.at[1], e3r.at[1], e_s.at[7], e_r.at[7], at_dn).wait_recv()
    enc = part[zh, c] + e1r[zh] + e3r[0].astype(F32) + e3r[1].astype(F32)
    average = jnp.mean(enc, axis=1, keepdims=True)
    centred = enc - average
    variance = jnp.mean(centred * centred, axis=1, keepdims=True)
    normed = (
        centred * lax.rsqrt(variance + layer_eps) * gain[...].reshape(1, E) + bias[...].reshape(1, E)
    ).astype(BF)
    for n in range(4):
        tgt[n] = normed[:, n * EC : (n + 1) * EC]
    for d in range(1, 8):
        to = (y + d) % 8
        go(remote(tgt.at[to % 4], table.at[seq, y], t_s.at[d], t_r.at[8 - d], {"head": to}))
    table[seq, y] = tgt[y % 4]
    relay(1)
    for d in range(1, 8):
        fr = (y + d) % 8
        remote(tgt.at[0], table.at[seq, fr], t_s.at[d], t_r.at[d], {"head": fr}).wait_recv()
    for w, where in enumerate((at_up, at_dn, at_sib)):
        go(remote(table.at[seq], table.at[seq], g_s.at[w], g_r.at[seq], where))
    finish(0)
    attend(0)
    relay(2)

    def took(s):
        remote(table.at[s], table.at[s], g_r.at[s], g_r.at[s], at_sib).wait_recv()

    took(s_dn)
    go(remote(table.at[s_dn, :4], table.at[s_dn, :4], g_s.at[3], g_r.at[s_dn], at_up))
    go(remote(table.at[s_dn], table.at[s_dn], g_s.at[4], g_r.at[s_dn], at_sib))
    took(s_up)
    go(remote(table.at[s_up, 4:], table.at[s_up, 4:], g_s.at[5], g_r.at[8], at_dn))
    go(remote(table.at[s_up], table.at[s_up], g_s.at[6], g_r.at[s_up], at_sib))
    finish(1)
    attend(1)
    finish(2)
    remote(table.at[s_op, :4], table.at[s_op, :4], g_s.at[3], g_r.at[s_op], at_up).wait_recv()
    remote(table.at[s_op, 4:], table.at[s_op, 4:], g_s.at[5], g_r.at[8], at_dn).wait_recv()
    go(remote(table.at[s_op], table.at[s_op], g_s.at[7], g_r.at[s_op], at_sib))
    attend(2)
    for z in range(4):
        took(z * 2 + o)
    picks = idx[...]
    spot = (picks % 128) // 16 * 128 + picks // 128 * 16 + picks % 16
    hot = (lax.broadcasted_iota(jnp.int32, (1024, TOK), 0) == spot).astype(F32).astype(BF)
    aligned[...] = lax.dot_general(
        hot, table[...].reshape(1024, EC), (((0,), (0,)), ((), ())), preferred_element_type=F32
    )
    for copy in sent:
        copy.wait_send()


def tail(
    attn, w, aligned, cos_out, grad_attn, grad_proj,
    part, a_sb, a_rb, b_sb, b_rb, stat, cosx, gp, r1s, r1r, own, r2s, r2r, r2h, r3s, r3r, r4s,
    ss_a, rs_a, ss_b, rs_b, ss_st, rs_st, ss_c, rs_c, ss_g, rs_g, ss_r, rs_r, ss_z, rs_z,
):
    x, zl, zh, c, y = places()
    th, ec = y // 4, y % 4
    odd = y % 2
    nxt, prv = (y + 1) % 8, (y + 7) % 8
    buddy = y + 2 * odd - 1
    buddy = (buddy + 8) % 8
    o = 1 - c
    at_sib = {"seq": zh * 2 + o}
    xu, xd, xo = (x + 1) % 4, (x + 3) % 4, (x + 2) % 4
    at_xu, at_xd = {"dp": xu * 2 + zl}, {"dp": xd * 2 + zl}
    sent = []

    def go(copy):
        copy.start()
        sent.append(copy)

    zpeers = []
    for d in range(1, 8):
        zz = (zh * 2 + zl + d) % 8
        zpeers.append({"dp": x * 2 + zz % 2, "seq": zz // 2 * 2 + c})
    greet([at_sib, at_xu, at_xd] + [{"head": (y + d) % 8} for d in range(1, 8)] + zpeers)

    partial = lax.dot_general(
        attn[...], w[...], (((1,), (1,)), ((), ())), preferred_element_type=F32
    )
    for i in range(PHASES):
        for t in range(2):
            for e in range(4):
                part[i, t * 4 + e] = partial[
                    t * HALF + i * SUB : t * HALF + (i + 1) * SUB, e * EC : (e + 1) * EC
                ]
    for i in range(PHASES):
        a_sb[i] = part[i, (y + 4) % 8].astype(BF)
        go(remote(a_sb.at[i], a_rb.at[i], ss_a.at[i], rs_a.at[i], {"head": buddy_of(y, odd)}))
    for i in range(PHASES):
        remote(a_sb.at[i], a_rb.at[i], ss_a.at[i], rs_a.at[i], {"head": nxt}).wait_recv()
        got = a_rb[i].astype(F32)
        far_p = part[i, (y + 3) % 8]
        far_m = part[i, (y + 5) % 8]
        b_sb[i, 0, 0] = jnp.where(odd == 1, far_p + got, far_p).astype(BF)
        b_sb[i, 0, 1] = jnp.where(odd == 1, far_m, far_m + got).astype(BF)
        go(remote(b_sb.at[i, 0, 0], b_rb.at[i, 0, 0], ss_b.at[i, 0, 0], rs_b.at[i, 0, 0], {"head": nxt}))
        go(remote(b_sb.at[i, 0, 1], b_rb.at[i, 0, 1], ss_b.at[i, 0, 1], rs_b.at[i, 0, 1], {"head": prv}))
    for s in range(1, 3):
        for i in range(PHASES):
            for side, where in ((0, nxt), (1, prv)):
                remote(b_sb.at[i, s - 1, side], b_rb.at[i, s - 1, side], ss_b.at[i, s - 1, side],
                       rs_b.at[i, s - 1, side], {"head": where}).wait_recv()
                to = (y + 3 - s) % 8 if side == 0 else (y + 5 + s) % 8
                b_sb[i, s, side] = (part[i, to] + b_rb[i, s - 1, side].astype(F32)).astype(BF)
                go(remote(b_sb.at[i, s, side], b_rb.at[i, s, side], ss_b.at[i, s, side],
                          rs_b.at[i, s, side], {"head": where}))

    def rows_of(i):
        return pl.ds(pl.multiple_of(th * HALF + i * SUB, 16), SUB)

    lane = lax.broadcasted_iota(jnp.int32, (128, 128), 1)
    sub = lax.broadcasted_iota(jnp.int32, (128, 128), 0)

    def fill(column):
        return jnp.concatenate([column, jnp.zeros((128 - SUB, 1), F32)], axis=0)

    for i in range(PHASES):
        for side, where in ((0, nxt), (1, prv)):
            remote(b_sb.at[i, 2, side], b_rb.at[i, 2, side], ss_b.at[i, 2, side],
                   rs_b.at[i, 2, side], {"head": where}).wait_recv()
        proj = part[i, y] + b_rb[i, 2, 0].astype(F32) + b_rb[i, 2, 1].astype(F32)
        part[i, y] = proj
        al = aligned[rows_of(i), :]
        pp = jnp.sum(proj * proj, axis=1, keepdims=True)
        pa = jnp.sum(proj * al, axis=1, keepdims=True)
        aa = jnp.sum(al * al, axis=1, keepdims=True)
        packed = jnp.where(lane == 0, fill(pp), jnp.where(lane == 1, fill(pa), jnp.where(lane == 2, fill(aa), 0.0)))
        stat[i, ec] = packed.T[0:8, :]
        for d in range(1, 4):
            to = th * 4 + (ec + d) % 4
            go(remote(stat.at[i, ec], stat.at[i, ec], ss_st.at[i, d], rs_st.at[i, 4 - d], {"head": to}))
    for i in range(PHASES):
        for d in range(1, 4):
            fr = (ec + d) % 4
            remote(stat.at[i, fr], stat.at[i, fr], ss_st.at[i, d], rs_st.at[i, d], {"head": th * 4 + fr}).wait_recv()
        total = stat[i, 0] + stat[i, 1] + stat[i, 2] + stat[i, 3]
        pp, pa, aa = total[0:1], total[1:2], total[2:3]
        pn = jnp.sqrt(pp + cos_eps)
        an = jnp.sqrt(aa + cos_eps)
        cos = pa / (pn * an)
        first = 1.0 / (pn * an)
        second = cos / (pn * pn)
        cosx[0, i : i + 1, :] = cos
        cols = jnp.where(sub == 0, first, jnp.where(sub == 1, second, 0.0)).T
        al = aligned[rows_of(i), :]
        gp[i, y] = (-(al * cols[:SUB, 0:1] - cols[:SUB, 1:2] * part[i, y])).astype(BF)
        for side, where in ((0, nxt), (1, prv)):
            go(remote(gp.at[i, y], gp.at[i, y], ss_g.at[i, side], rs_g.at[i, side], {"head": where}))
    go(remote(cosx.at[0], cosx.at[1], ss_c.at[0], rs_c.at[0], {"head": (y + 4) % 8}))

    for s in range(1, 3):
        for i in range(PHASES):
            for side, where in ((0, nxt), (1, prv)):
                src = (y + 8 - s) % 8 if side == 0 else (y + s) % 8
                n = 2 * (s - 1) + side
                remote(gp.at[i, src], gp.at[i, src], ss_g.at[i, n], rs_g.at[i, n], {"head": where}).wait_recv()
                go(remote(gp.at[i, src], gp.at[i, src], ss_g.at[i, n + 2], rs_g.at[i, n + 2], {"head": where}))
    for i in range(PHASES):
        for side, where in ((0, nxt), (1, prv)):
            src = (y + 5) % 8 if side == 0 else (y + 3) % 8
            n = 4 + side
            remote(gp.at[i, src], gp.at[i, src], ss_g.at[i, n], rs_g.at[i, n], {"head": where}).wait_recv()
        src = (y + 3 + 2 * odd) % 8
        go(remote(gp.at[i, src], gp.at[i, src], ss_g.at[i, 6], rs_g.at[i, 6], {"head": buddy_of(y, 1 - odd)}))
    for i in range(PHASES):
        src = (y + 4) % 8
        remote(gp.at[i, src], gp.at[i, src], ss_g.at[i, 6], rs_g.at[i, 6], {"head": nxt}).wait_recv()

    full = jnp.concatenate(
        [
            jnp.concatenate([gp[i, t * 4 + e] for e in range(4)], axis=1)
            for t in range(2)
            for i in range(PHASES)
        ],
        axis=0,
    )
    attn_v = attn[...]
    grad = lax.dot_general(full, attn_v, (((0,), (0,)), ((), ())), preferred_element_type=F32)
    for xx in range(4):
        for zz in range(2):
            own[xx, zz] = grad[xx * EC + zz * 192 : xx * EC + (zz + 1) * 192]
    for xx in range(4):
        r1s[xx] = own[xx, o].astype(BF)
        go(remote(r1s.at[xx], r1r.at[xx], ss_r.at[xx], rs_r.at[xx], at_sib))
    grad_attn[...] = jnp.dot(full, w[...], preferred_element_type=F32).astype(BF)
    for xx in range(4):
        remote(r1s.at[xx], r1r.at[xx], ss_r.at[xx], rs_r.at[xx], at_sib).wait_recv()
    far = own[xo, c] + r1r[xo].astype(F32)
    r2h[0] = far[:96].astype(BF)
    r2h[1] = far[96:].astype(BF)
    go(remote(r2h.at[0], r2h.at[2], ss_r.at[4], rs_r.at[4], at_xu))
    go(remote(r2h.at[1], r2h.at[3], ss_r.at[5], rs_r.at[5], at_xd))
    near_u = own[xu, c] + r1r[xu].astype(F32)
    near_d = own[xd, c] + r1r[xd].astype(F32)
    r2s[0, 96:] = near_u[96:].astype(BF)
    r2s[1, :96] = near_d[:96].astype(BF)
    mine = own[x, c] + r1r[x].astype(F32)
    remote(r2h.at[0], r2h.at[2], ss_r.at[4], rs_r.at[4], at_xu).wait_recv()
    r2s[0, :96] = (near_u[:96] + r2h[2].astype(F32)).astype(BF)
    go(remote(r2s.at[0], r2r.at[0], ss_r.at[6], rs_r.at[6], at_xu))
    remote(r2h.at[1], r2h.at[3], ss_r.at[5], rs_r.at[5], at_xd).wait_recv()
    r2s[1, 96:] = (near_d[96:] + r2h[3].astype(F32)).astype(BF)
    go(remote(r2s.at[1], r2r.at[1], ss_r.at[7], rs_r.at[7], at_xd))
    remote(r2s.at[0], r2r.at[0], ss_r.at[6], rs_r.at[6], at_xu).wait_recv()
    remote(r2s.at[1], r2r.at[1], ss_r.at[7], rs_r.at[7], at_xd).wait_recv()
    mine = mine + r2r[0].astype(F32) + r2r[1].astype(F32)

    for n in range(4):
        r3s[n] = mine[n * SUB : (n + 1) * SUB].astype(BF)
    pos = zh * 2 + zl
    for d in range(1, 8):
        to = (pos + d) % 8
        copy = remote(r3s.at[to // 2], r3r.at[d], ss_z.at[d], rs_z.at[d],
                      {"dp": x * 2 + to % 2, "seq": to // 2 * 2 + c})

        @pl.when(to % 2 == c)
        def _(copy=copy):
            copy.start()

    @pl.when(zl == c)
    def _():
        acc = r3s[zh].astype(F32)
        for d in range(1, 8):
            remote(r3s.at[0], r3r.at[d], ss_z.at[d], rs_z.at[d], at_sib).wait_recv()
            acc = acc + r3r[d].astype(F32)
        r4s[0] = acc[:24]
        r4s[1] = acc[24:]
        copy = remote(r4s.at[o], r4s.at[2], ss_r.at[8], rs_r.at[8], at_sib)
        copy.start()
        grad_proj[...] = r4s[c]
        copy.wait_send()

    remote(cosx.at[0], cosx.at[1], ss_c.at[0], rs_c.at[0], {"head": (y + 4) % 8}).wait_recv()
    row = jnp.zeros((8, 384), F32)
    token = lax.broadcasted_iota(jnp.int32, (8, 384), 1)
    for n in range(2):
        start = (th + (1 - 2 * th) * n) * HALF
        for i in range(PHASES):
            wide = jnp.concatenate(
                [jnp.broadcast_to(cosx[n, i : i + 1, :], (8, 128)), jnp.zeros((8, 256), F32)], axis=1
            )
            moved = pltpu.roll(wide, start + i * SUB, 1)
            row = jnp.where((token >= start + i * SUB) & (token < start + (i + 1) * SUB), moved, row)
    cos_out[...] = row[0:1, :TOK]

    @pl.when(zl != c)
    def _():
        remote(r4s.at[0], r4s.at[2], ss_r.at[8], rs_r.at[8], at_sib).wait_recv()
        grad_proj[...] = r4s[2]

    for d in range(1, 8):
        to = (pos + d) % 8
        copy = remote(r3s.at[to // 2], r3r.at[d], ss_z.at[d], rs_z.at[d],
                      {"dp": x * 2 + to % 2, "seq": to // 2 * 2 + c})

        @pl.when(to % 2 == c)
        def _(copy=copy):
            copy.wait_send()

    for copy in sent:
        copy.wait_send()


def buddy_of(y, odd):
    return (y + 1 + 6 * odd) % 8


def on_device(patch_in, enc_weight, enc_gain, enc_bias, interp_index, queries, key_rows, value_rows, proj_weight):
    vm = pl.BlockSpec(memory_space=pltpu.VMEM)
    dma = pltpu.SemaphoreType.DMA
    attn, aligned = pl.pallas_call(
        front,
        out_shape=(jax.ShapeDtypeStruct((TOK, DA), BF), jax.ShapeDtypeStruct((TOK, EC), F32)),
        in_specs=[vm] * 8,
        out_specs=(vm, vm),
        scratch_shapes=[
            pltpu.VMEM((NH, 8, TOK, HD), BF),
            pltpu.VMEM((NH, 8, TOK, HD), BF),
            pltpu.VMEM((4, 2, 16, E), F32),
            pltpu.VMEM((4, 16, E), F32),
            pltpu.VMEM((2, 16, E // 2), BF),
            pltpu.VMEM((2, 16, E // 2), BF),
            pltpu.VMEM((2, 16, E), BF),
            pltpu.VMEM((2, 16, E), BF),
            pltpu.VMEM((4, 16, EC), BF),
            pltpu.VMEM((8, 8, 16, EC), BF),
            dma((NH, 7)),
            dma((NH, 8)),
            dma((NH, 7)),
            dma((NH, 8)),
            dma((8,)),
            dma((8,)),
            dma((8,)),
            dma((8,)),
            dma((8,)),
            dma((9,)),
        ],
        compiler_params=pltpu.CompilerParams(
            collective_id=0, has_side_effects=True, vmem_limit_bytes=48 * 2**20
        ),
        name="front",
    )(
        patch_in[0],
        enc_weight,
        enc_gain,
        enc_bias,
        interp_index,
        queries[0],
        key_rows[0],
        value_rows[0],
    )
    cosine, grad_attn, grad_proj = pl.pallas_call(
        tail,
        out_shape=(
            jax.ShapeDtypeStruct((1, TOK), F32),
            jax.ShapeDtypeStruct((TOK, DA), BF),
            jax.ShapeDtypeStruct((24, DA), F32),
        ),
        in_specs=[vm] * 3,
        out_specs=(vm, vm, vm),
        scratch_shapes=[
            pltpu.VMEM((PHASES, 8, SUB, EC), F32),
            pltpu.VMEM((PHASES, SUB, EC), BF),
            pltpu.VMEM((PHASES, SUB, EC), BF),
            pltpu.VMEM((PHASES, 3, 2, SUB, EC), BF),
            pltpu.VMEM((PHASES, 3, 2, SUB, EC), BF),
            pltpu.VMEM((PHASES, 4, 8, 128), F32),
            pltpu.VMEM((2, 8, 128), F32),
            pltpu.VMEM((PHASES, 8, SUB, EC), BF),
            pltpu.VMEM((4, 192, DA), BF),
            pltpu.VMEM((4, 192, DA), BF),
            pltpu.VMEM((4, 2, 192, DA), F32),
            pltpu.VMEM((2, 192, DA), BF),
            pltpu.VMEM((2, 192, DA), BF),
            pltpu.VMEM((4, 96, DA), BF),
            pltpu.VMEM((4, SUB, DA), BF),
            pltpu.VMEM((8, SUB, DA), BF),
            pltpu.VMEM((3, 24, DA), F32),
            dma((PHASES,)),
            dma((PHASES,)),
            dma((PHASES, 3, 2)),
            dma((PHASES, 3, 2)),
            dma((PHASES, 4)),
            dma((PHASES, 4)),
            dma((1,)),
            dma((1,)),
            dma((PHASES, 7)),
            dma((PHASES, 7)),
            dma((9,)),
            dma((9,)),
            dma((8,)),
            dma((8,)),
        ],
        compiler_params=pltpu.CompilerParams(
            collective_id=1, has_side_effects=True, vmem_limit_bytes=48 * 2**20
        ),
        name="tail",
    )(attn, proj_weight, aligned)
    return attn[None], cosine, grad_attn[None], grad_proj


def solution(mesh):
    placed = (
        P("dp", "head", "seq"),
        P("seq", None),
        P(),
        P(),
        P("dp", "seq"),
        P("dp", "seq", "head"),
        P("dp", "seq", "head"),
        P("dp", "seq", "head"),
        P(None, "head"),
    )
    return jax.shard_map(
        on_device,
        mesh=mesh,
        in_specs=placed,
        out_specs=(
            P("dp", "seq", "head"),
            P("dp", "seq"),
            P("dp", "seq", "head"),
            P(("dp", "seq"), "head"),
        ),
        check_vma=False,
    )
```

time: 577 us -> 130 us (0.23)
  waiting for transfers between devices: 523 us -> 0 us
  Pallas kernels: 0 us -> 120 us
  matrix products: 14.5 us -> 0 us
  between operations: 14.3 us -> 0.69 us
  other arithmetic: 9.87 us -> 0 us
    unnamed x7 -> x0, waiting for transfers between devices: 263 us -> none
    all_gather x3 -> x0, waiting for transfers between devices: 146 us -> none  [the longest x1 80 us: on_device(): lax.all_gather(targets, ('seq', 'head'), axis=0, tiled=True)]
    pallas_call x0 -> x2, Pallas kernels: none -> 120 us  [the longest x1 63.2 us: on_device(): pl.pallas_call(tail, out_shape=(jax.ShapeDtypeStruct((1, TOK), F32), jax....]
    psum x1 -> x0, waiting for transfers between devices: 68.5 us -> none  [on_device(): lax.psum(partial_proj.astype(jnp.bfloat16), 'head').astype(jnp.float32)]
    reduce_scatter x1 -> x0, waiting for transfers between devices: 45.2 us -> none  [on_device(): lax.psum_scatter(jnp.dot(local_patches, enc_weight, preferred_element_typ...]
    dot_general x10 -> x0, matrix products: 14.5 us -> none  [the longest x3 3.81 us: on_device(): head_outs.append(jnp.dot(probs, v_head, preferred_element_type=jnp.float32))]
    gather x1 -> x0, local copies, waits for them, and re-layouts: 5.96 us -> none  [pick_rows(): jnp.take(portion, jnp.clip(row_of_token, 0, portion.shape[0] - 1), axis=0)]
  transfers between devices with their start and end apart: 6 -> 0, of which waited for: 6 -> 0; matrix products, arithmetic and copies ran while one was open for 4% -> 0% of each run, Pallas kernels for 0% -> 0%
where the time goes in v1:
time: 130 us
  Pallas kernels  120 us (92%)
  local copies, waits for them, and re-layouts  9.48 us (7%)
    pallas_call x1, Pallas kernels, on_device(): pl.pallas_call(tail, out_shape=(jax.ShapeDtypeStruct((1, TOK), F32), jax....  63.2 us
    pallas_call x1, Pallas kernels, on_device(): pl.pallas_call(front, out_shape=(jax.ShapeDtypeStruct((TOK, DA), BF), jax...  56.7 us
    unnamed x21, local copies, waits for them, and re-layouts  9.48 us

profile of v1, /device:TPU:1, one launch (start us, length us, event | category | flops | bytes accessed | tf_op | source)
XLA Modules:
  0.0 130.0 jit_solution(15481287390076710657)
XLA Ops:
  0.6 0.0 copy-start
  0.6 1.0 copy.13
  1.6 0.0 copy-start.1
  1.7 1.1 copy-done.1
  2.7 0.0 copy-start.2
  2.7 0.9 copy-done.2
  3.6 0.0 copy-start.3
  3.6 0.9 copy-done.3
  4.6 0.0 copy-start.4
  4.6 0.9 copy-done.4
  5.5 0.0 copy-start.5
  5.5 0.7 copy-done.5
  6.2 0.0 copy-start.6
  6.2 0.7 copy-done.6
  6.9 0.0 copy-start.7
  6.9 0.7 copy-done.7
  7.6 56.7 %front.1 = (bf16[288,384]{1,0:T(8,128)(2,1)S(1)}, f32[288,384]{1,0:T(8,128)S(1)}) custom-call(bf16[128,192]{1,0:T(8,128)(2,1)S(1)} %bitcast.7, bf16[192,1536]{1,0:T(8,128)(2,1)S(1)} %copy-done.1, f32[1536]{0:T(1024)S(1)} %copy-done.5, f32[1536]{0:T(1024)S(1)} %copy-done.6, s32[1,288]{1,0:T(1,128)S(1)} %copy-done.7, bf16[288,384]{1,0:T(8,128)(2,1)S(1)} %bitcast.9, ...), custom_call_target="tpu_custom_call" | custom-call | tf_op jit(solution)/shard_map/front/pallas_call | solution.py:418
  64.3 0.0 copy-done
  64.3 63.2 %tail.1 = (f32[1,288]{1,0:T(1,128)S(1)}, bf16[288,384]{1,0:T(8,128)(2,1)S(1)}, f32[24,384]{1,0:T(8,128)S(1)}) custom-call(bf16[288,384]{1,0:T(8,128)(2,1)S(1)} %get-tuple-element.9.attn, bf16[1536,384]{1,0:T(8,128)(2,1)S(1)} %copy-done, f32[288,384]{1,0:T(8,128)S(1)} %get-tuple-element.10.aligned), custom_call_target="tpu_custom_call" | custom-call | tf_op jit(solution)/shard_map/tail/pallas_call | solution.py:459
  127.5 0.7 copy.18
  128.2 0.6 copy.19
  128.7 0.7 copy.20
  129.4 0.6 copy.21
Async XLA Ops:
  0.6 63.6 %copy-start = (bf16[1536,384]{1,0:T(8,128)(2,1)S(1)}, bf16[1536,384]{1,0:T(8,128)(2,1)}, u32[]{:S(2)}) copy-start(bf16[1536,384]{1,0:T(8,128)(2,1)} %w.1) | copy-start | bytes 3538948
  1.6 1.1 copy-start.1
  2.7 0.9 copy-start.2
  3.6 0.9 copy-start.3
  4.6 0.9 copy-start.4
  5.5 0.7 copy-start.5
  6.2 0.7 copy-start.6
  6.9 0.7 copy-start.7

commit v2 on v0

v2 whole, which is shorter than its diff:
```python
import jax
import jax.numpy as jnp
from jax import lax
from jax.experimental import pallas as pl
from jax.experimental.pallas import tpu as pltpu
from jax.sharding import PartitionSpec as P

MESH = pl.DeviceIdType.MESH
BF = jnp.bfloat16
F32 = jnp.float32

E = 1536
HD = 128
NH = 3
DA = NH * HD
TOK = 288
SUB = 48
EC = 384
PH = 3
PT = 2 * SUB
BLK = 192

layer_eps = 1e-06
cos_eps = 1e-06
EXP_SCALE = HD**-0.5 * 1.4426950408889634


def remote(src, dst, send, recv, where):
    return pltpu.make_async_remote_copy(
        src_ref=src, dst_ref=dst, send_sem=send, recv_sem=recv, device_id=where, device_id_type=MESH
    )


def kernel(
    patch_h, enc_h, gain_h, bias_h, idx_h, q_h, k_h, v_h, w_h,
    attn, cos_out, grad_attn, grad_proj,
    patch, enc_w, gain, bias, idx, w, q3, k3, v3,
    qb, kb, vb, ob, at3, part, e1r, e2s, e2r, tn, tb, aligned,
    pp, s1, r1, sf, rf, s2, r2, pr, stat, cosx,
    own, g1s, g1r, g2s, g2r, g3s, g3r,
    l_s, l3_s, k_s, k_r, ks_s, ks_r, v_s, v_r, vs_s, vs_r, q_s, q_r, o_s, o_r, e_s, e_r, t_s, t_r, ty_s, ty_r, tc_s, tc_r,
    p_s, p_r, st_s, st_r, c_s, c_r, a_s, a_r, g_s, g_r, z_s, z_r,
):
    dp, seq, y = lax.axis_index("dp"), lax.axis_index("seq"), lax.axis_index("head")
    x, zl, zh, c = dp // 2, dp % 2, seq // 2, seq % 2
    o = 1 - c
    odd = y % 2
    half, chunk = y // 4, y % 4
    pos = zh * 2 + zl
    at_sib = {"seq": zh * 2 + o}
    sent = []

    def at_y(d):
        return {"head": (y + d) % 8}

    def go(copy):
        copy.start()
        sent.append(copy)

    loads = [
        pltpu.make_async_copy(src, dst, l_s.at[n])
        for n, (src, dst) in enumerate(
            ((patch_h, patch), (enc_h, enc_w), (gain_h, gain), (bias_h, bias), (idx_h, idx), (w_h, w))
        )
    ]
    qkv_loads = [
        [
            pltpu.make_async_copy(src.at[:, h * HD : (h + 1) * HD], dst.at[h], l3_s.at[n, h])
            for h in range(NH)
        ]
        for n, (src, dst) in enumerate(((k_h, k3), (v_h, v3), (q_h, q3)))
    ]
    for copy in (*loads[:2], *qkv_loads[0], *qkv_loads[1], *qkv_loads[2], *loads[2:]):
        copy.start()

    barrier = pltpu.get_barrier_semaphore()
    peers = [at_y(d) for d in range(1, 8)]
    peers += [{"dp": (x + d) % 4 * 2 + zl} for d in (1, 2, 3)]
    peers += [at_sib]
    for d in range(1, 8):
        to = (pos + d) % 8
        for cc in range(2):
            peers.append({"dp": x * 2 + to % 2, "seq": to // 2 * 2 + cc})
    for peer in peers:
        pl.semaphore_signal(barrier, inc=1, device_id=peer, device_id_type=MESH)
    pl.semaphore_wait(barrier, len(peers))

    first = 2 * zl + 1
    mine_r = (zh + 4 - first) % 4
    active = mine_r < NH
    workers = [(first + r) % 4 for r in range(NH)]
    cond_sent = []

    def go_if(cond, copy):
        cond_sent.append((cond, copy))

        @pl.when(cond)
        def _():
            copy.start()

    def scatter(src, buf, ss, rs):
        for r, worker in enumerate(workers):
            go_if(worker != zh, remote(src.at[r], buf.at[seq], ss.at[r], rs.at[zh], {"seq": worker * 2 + c}))

    def to_sib(buf, ss, rs, z):
        copy = remote(buf.at[z * 2 + c], buf.at[z * 2 + c], ss.at[z], rs.at[z], at_sib)
        copy.start()
        return copy

    def keep(src, buf, ss, rs):
        @pl.when(active)
        def _():
            buf[seq] = src[mine_r]
            to_sib(buf, ss, rs, zh)

    def pass_on(buf, rs, ss2, rs2):
        @pl.when(active)
        def _():
            for d in (1, 3, 2):
                z = (zh + d) % 4
                remote(buf.at[z * 2 + c], buf.at[z * 2 + c], rs.at[z], rs.at[z], at_sib).wait_recv()
                to_sib(buf, ss2, rs2, z)

    loads[0].wait()
    loads[1].wait()
    share = lax.dot_general(
        patch[...], enc_w[...], (((0,), (0,)), ((), ())), preferred_element_type=F32
    )
    for z in range(4):
        for cc in range(2):
            part[cc, z] = share[(2 * z + cc) * 16 : (2 * z + cc + 1) * 16]
    e1 = remote(part.at[o], e1r, e_s.at[0], e_r.at[0], at_sib)
    go(e1)
    for copy in qkv_loads[0]:
        copy.wait()
    scatter(k3, kb, k_s, k_r)
    keep(k3, kb, ks_s, ks_r)
    e1.wait_recv()
    for d in (2, 1, 3):
        to = (zh + d) % 4
        e2s[d] = (part[c, to] + e1r[to]).astype(BF)
        go(remote(e2s.at[d], e2r.at[4 - d], e_s.at[d], e_r.at[4 - d], {"seq": to * 2 + c}))
    for copy in qkv_loads[1]:
        copy.wait()
    scatter(v3, vb, v_s, v_r)
    keep(v3, vb, vs_s, vs_r)
    enc = part[c, zh] + e1r[zh]
    for d in (1, 2, 3):
        remote(e2s.at[d], e2r.at[d], e_s.at[d], e_r.at[d], at_sib).wait_recv()
        enc = enc + e2r[d].astype(F32)
    loads[2].wait()
    loads[3].wait()
    average = jnp.mean(enc, axis=1, keepdims=True)
    centred = enc - average
    variance = jnp.mean(centred * centred, axis=1, keepdims=True)
    normed = (
        centred * lax.rsqrt(variance + layer_eps) * gain[...].reshape(1, E) + bias[...].reshape(1, E)
    ).astype(BF)
    for e in range(4):
        tn[e, zh] = normed[:, e * EC : (e + 1) * EC]
    for d in (2, 1, 3):
        to = (zh + d) % 4
        go(remote(tn.at[:, zh], tn.at[:, zh], t_s.at[d], t_r.at[4 - d], {"seq": to * 2 + c}))
    for copy in qkv_loads[2]:
        copy.wait()
    for i in range(PH):
        rows = slice(i * PT, (i + 1) * PT)
        for r, worker in enumerate(workers):
            go_if(
                worker != zh,
                remote(q3.at[r, rows], qb.at[i, zh], q_s.at[i, r], q_r.at[i, zh], {"seq": worker * 2 + c}),
            )
    pass_on(kb, k_r, ks_s, ks_r)
    for d in (1, 2, 3):
        fr = (zh + d) % 4
        remote(tn.at[:, fr], tn.at[:, fr], t_s.at[d], t_r.at[d], at_sib).wait_recv()
    for d in (4, 3, 5, 2, 6, 1, 7):
        go(remote(tn.at[(y + d) % 4], tb.at[y, c], ty_s.at[d], ty_r.at[8 - d], at_y(d)))
    tb[y, c] = tn[chunk]

    def gather_start(at, ss, rs):
        for n, d in enumerate((2, 6, 1, 7)):
            go(remote(at(y), at(y), ss(n), rs(8 - d), at_y(d)))

    def gather_took(at, rs, d):
        fr = (y + d) % 8
        remote(at(fr), at(fr), rs(d), rs(d), at_y(d)).wait_recv()

    def gather_relay(at, ss, rs):
        gather_took(at, rs, 6)
        lo = (y + 6) % 8
        gather_took(at, rs, 2)
        hi = (y + 2) % 8
        far = (y + 6 + 4 * odd) % 8
        go(remote(at(far), at(far), ss(6), rs(4), at_y(2 + 4 * odd)))
        go(remote(at(lo), at(lo), ss(4), rs(5), at_y(1)))
        go(remote(at(hi), at(hi), ss(5), rs(3), at_y(7)))

    pass_on(vb, v_r, vs_s, vs_r)

    @pl.when(active)
    def _():
        for buf, rs in ((kb, ks_r), (vb, vs_r)):
            for z in range(4):
                remote(buf.at[z * 2 + o], buf.at[z * 2 + o], rs.at[z], rs.at[z], at_sib).wait_recv()
        for i in range(PH):
            rows = slice(i * PT, (i + 1) * PT)
            qb[i, zh] = q3[mine_r, rows]
            for d in (1, 3, 2):
                z = (zh + d) % 4
                remote(qb.at[i, z], qb.at[i, z], q_r.at[i, z], q_r.at[i, z], at_sib).wait_recv()
            scores = lax.dot_general(
                qb[i].reshape(4 * PT, HD), kb[...].reshape(8 * TOK, HD), (((1,), (1,)), ((), ())),
                preferred_element_type=F32,
            )
            top = jnp.max(scores, axis=1, keepdims=True)
            expo = jnp.exp2((scores - top) * EXP_SCALE).astype(BF)
            wide = jnp.concatenate([vb[...].reshape(8 * TOK, HD), jnp.ones((8 * TOK, HD), BF)], axis=1)
            out = jnp.dot(expo, wide, preferred_element_type=F32)
            ob[i] = (out[:, :HD] / out[:, HD:]).astype(BF).reshape(4, PT, HD)
            for d in (2, 1, 3):
                z = (zh + d) % 4
                remote(ob.at[i, z], at3.at[mine_r, rows], o_s.at[i, d], o_r.at[mine_r, i], {"seq": z * 2 + c}).start()
            at3[mine_r, rows] = ob[i, zh]

    loads[5].wait()

    for i in range(PH):
        rows = slice(i * PT, (i + 1) * PT)
        for r, worker in enumerate(workers):

            @pl.when(worker != zh)
            def _(r=r, rows=rows, i=i):
                remote(at3.at[r, rows], at3.at[r, rows], o_r.at[r, i], o_r.at[r, i], at_sib).wait_recv()

        attn[rows, :] = jnp.concatenate([at3[r, rows] for r in range(NH)], axis=1)
        partial = lax.dot_general(
            attn[rows, :], w[...], (((1,), (1,)), ((), ())), preferred_element_type=F32
        )
        for t in range(2):
            for e in range(4):
                pp[i, t * 4 + e] = partial[t * SUB : (t + 1) * SUB, e * EC : (e + 1) * EC]
        sf[i] = pp[i, (y + 4) % 8].astype(BF)
        go(remote(sf.at[i], rf.at[i], p_s.at[i, 0], p_r.at[i, 0], at_y(2 + 4 * odd)))
        s1[i, 0, 1] = pp[i, (y + 3) % 8].astype(BF)
        s1[i, 0, 0] = pp[i, (y + 1) % 8].astype(BF)
        go(remote(s1.at[i, 0], r1.at[i, 0], p_s.at[i, 1], p_r.at[i, 1], at_y(1)))
        s1[i, 1, 1] = pp[i, (y + 5) % 8].astype(BF)
        s1[i, 1, 0] = pp[i, (y + 7) % 8].astype(BF)
        go(remote(s1.at[i, 1], r1.at[i, 1], p_s.at[i, 2], p_r.at[i, 2], at_y(7)))
    for d in range(1, 8):
        fr = (y + d) % 8
        remote(tb.at[fr, c], tb.at[fr, c], ty_s.at[d], ty_r.at[d], at_y(d)).wait_recv()
    to_core = remote(tb.at[:, c], tb.at[:, c], tc_s.at[0], tc_r.at[0], at_sib)
    go(to_core)
    for i in range(PH):
        remote(sf.at[i], rf.at[i], p_s.at[i, 0], p_r.at[i, 0], at_y(1)).wait_recv()
        remote(s1.at[i, 0], r1.at[i, 0], p_s.at[i, 1], p_r.at[i, 1], at_y(1)).wait_recv()
        remote(s1.at[i, 1], r1.at[i, 1], p_s.at[i, 2], p_r.at[i, 2], at_y(7)).wait_recv()
        far = rf[i].astype(F32)
        upper = pp[i, (y + 2) % 8] + r1[i, 0, 1].astype(F32)
        lower = pp[i, (y + 6) % 8] + r1[i, 1, 1].astype(F32)
        s2[i, 0] = jnp.where(odd == 0, upper + far, upper).astype(BF)
        go(remote(s2.at[i, 0], r2.at[i, 0], p_s.at[i, 3], p_r.at[i, 3], at_y(2)))
        s2[i, 1] = jnp.where(odd == 1, lower + far, lower).astype(BF)
        go(remote(s2.at[i, 1], r2.at[i, 1], p_s.at[i, 4], p_r.at[i, 4], at_y(6)))

    loads[4].wait()
    picks = idx[...]
    rest = picks % 128
    spot = picks // 128 * 128 + rest // 16 % 2 * 64 + rest // 32 * 16 + rest % 16
    hot = (lax.broadcasted_iota(jnp.int32, (1024, TOK), 0) == spot).astype(F32).astype(BF)
    remote(tb.at[:, o], tb.at[:, o], tc_s.at[0], tc_r.at[0], at_sib).wait_recv()
    aligned[...] = lax.dot_general(
        hot, tb[...].reshape(1024, EC), (((0,), (0,)), ((), ())), preferred_element_type=F32
    )

    lane = lax.broadcasted_iota(jnp.int32, (128, 128), 1)
    sub = lax.broadcasted_iota(jnp.int32, (128, 128), 0)

    def tall(column):
        return jnp.concatenate([column, jnp.zeros((128 - SUB, 1), F32)], axis=0)

    def own_rows(i):
        return pl.ds(pl.multiple_of(i * PT + half * SUB, 16), SUB)

    for i in range(PH):
        remote(s2.at[i, 0], r2.at[i, 0], p_s.at[i, 3], p_r.at[i, 3], at_y(2)).wait_recv()
        remote(s2.at[i, 1], r2.at[i, 1], p_s.at[i, 4], p_r.at[i, 4], at_y(6)).wait_recv()
        proj = (
            pp[i, y]
            + (r1[i, 0, 0].astype(F32) + r1[i, 1, 0].astype(F32))
            + (r2[i, 0].astype(F32) + r2[i, 1].astype(F32))
        )
        pp[i, y] = proj
        al = aligned[own_rows(i), :]
        sums = [jnp.sum(v, axis=1, keepdims=True) for v in (proj * proj, proj * al, al * al)]
        packed = jnp.where(
            lane == 0, tall(sums[0]), jnp.where(lane == 1, tall(sums[1]), jnp.where(lane == 2, tall(sums[2]), 0.0))
        )
        stat[i, chunk] = packed.T[0:8, :]
        for d in (2, 1, 3):
            to = half * 4 + (chunk + d) % 4
            go(remote(stat.at[i, chunk], stat.at[i, chunk], st_s.at[i, d], st_r.at[i, 4 - d], {"head": to}))

    def grad_at(i):
        return (lambda n: pr.at[i, n]), (lambda n: a_s.at[i, n]), (lambda n: a_r.at[i, n])

    for i in range(PH):
        for d in (1, 2, 3):
            fr = (chunk + d) % 4
            remote(stat.at[i, fr], stat.at[i, fr], st_s.at[i, d], st_r.at[i, d], at_sib).wait_recv()
        total = (stat[i, 0] + stat[i, 1]) + (stat[i, 2] + stat[i, 3])
        pn = jnp.sqrt(total[0:1] + cos_eps)
        an = jnp.sqrt(total[2:3] + cos_eps)
        cos = total[1:2] / (pn * an)
        cosx[0, i] = jnp.broadcast_to(cos, (8, 128))
        factors = jnp.where(sub == 0, 1.0 / (pn * an), jnp.where(sub == 1, cos / (pn * pn), 0.0)).T
        al = aligned[own_rows(i), :]
        pr[i, y] = (-(al * factors[:SUB, 0:1] - factors[:SUB, 1:2] * pp[i, y])).astype(BF)
        gather_start(*grad_at(i))
    go(remote(cosx.at[0], cosx.at[1], c_s.at[0], c_r.at[0], at_y(4)))
    for i in range(PH):
        gather_relay(*grad_at(i))
    for i in range(PH):
        at, ss, rs = grad_at(i)
        for d in (1, 7, 3, 5, 4):
            gather_took(at, rs, d)

    def grad_columns(e):
        return jnp.concatenate([pr[i, t * 4 + e] for i in range(PH) for t in range(2)], axis=0)

    xo, xu, xd = (x + 2) % 4, (x + 1) % 4, (x + 3) % 4
    for n, xx in enumerate((xo, xu, xd, x)):
        block = lax.dot_general(grad_columns(xx), attn[...], (((0,), (0,)), ((), ())), preferred_element_type=F32)
        for zz in range(2):
            own[xx, zz] = block[zz * BLK : (zz + 1) * BLK]
        g1s[n] = own[xx, o].astype(BF)
        go(remote(g1s.at[n], g1r.at[n], g_s.at[n], g_r.at[n], at_sib))
    for n, (xx, d) in enumerate(((xo, 2), (xu, 1), (xd, 3))):
        remote(g1s.at[n], g1r.at[n], g_s.at[n], g_r.at[n], at_sib).wait_recv()
        g2s[n] = (own[xx, c] + g1r[n].astype(F32)).astype(BF)
        go(remote(g2s.at[n], g2r.at[4 - d], g_s.at[3 + d], g_r.at[8 - d], {"dp": xx * 2 + zl}))
    back = jnp.dot(grad_columns(0), w[:EC], preferred_element_type=F32)
    for e in range(1, 4):
        back = back + jnp.dot(grad_columns(e), w[e * EC : (e + 1) * EC], preferred_element_type=F32)
    grad_attn[...] = back.astype(BF)
    remote(g1s.at[3], g1r.at[3], g_s.at[3], g_r.at[3], at_sib).wait_recv()
    mine = own[x, c] + g1r[3].astype(F32)
    for d in (1, 3, 2):
        remote(g2s.at[0], g2r.at[d], g_s.at[3 + d], g_r.at[4 + d], {"dp": xu * 2 + zl}).wait_recv()
        mine = mine + g2r[d].astype(F32)
    for n in range(8):
        g3s[n] = jnp.concatenate([mine[n * 24 : (n + 1) * 24], jnp.zeros((8, DA), F32)], axis=0).astype(BF)
    z_sends = []
    for dz in range(4):
        for cc in range(2):
            to = (zh + dz) % 4
            copy = remote(g3s.at[to * 2 + cc], g3r.at[pos], z_s.at[dz, cc], z_r.at[pos],
                          {"dp": x * 2 + c, "seq": to * 2 + cc})
            if dz == 0:
                away = (zl != c) | (c != cc)
                z_sends.append((copy, away))

                @pl.when(away)
                def _(copy=copy):
                    copy.start()
            else:
                go(copy)
    row = jnp.zeros((8, 384), F32)
    token = lax.broadcasted_iota(jnp.int32, (8, 384), 1)
    remote(cosx.at[0], cosx.at[1], c_s.at[0], c_r.at[0], at_y(4)).wait_recv()
    for n in range(2):
        for i in range(PH):
            start = i * PT + (half + (1 - 2 * half) * n) * SUB
            wide = jnp.concatenate([cosx[n, i], jnp.zeros((8, 256), F32)], axis=1)
            inside = (token >= start) & (token < start + SUB)
            row = jnp.where(inside, pltpu.roll(wide, start, 1), row)
    cos_out[...] = row[0:1, :TOK]

    @pl.when(zl == c)
    def _():
        g3r[pos] = g3s[zh * 2 + c]

    @pl.when(zl != c)
    def _():
        remote(g3s.at[0], g3r.at[pos], z_s.at[0, 0], z_r.at[pos], at_sib).wait_recv()

    for d in range(1, 8):
        fr = (pos + d) % 8
        remote(g3s.at[0], g3r.at[fr], z_s.at[0, 0], z_r.at[fr], at_sib).wait_recv()
    total = g3r[0].astype(F32)
    for n in range(1, 8):
        total = total + g3r[n].astype(F32)
    grad_proj[...] = total[:24]

    @pl.when(active)
    def _():
        for z in range(4):
            for buf, ss in ((kb, ks_s), (vb, vs_s)):
                remote(buf.at[z * 2 + c], buf.at[z * 2 + c], ss.at[z], ks_r.at[z], at_sib).wait_send()
        for i in range(PH):
            for d in (1, 2, 3):
                remote(ob.at[i, d], at3.at[0, :PT], o_s.at[i, d], o_r.at[0, i], at_sib).wait_send()

    for cond, copy in cond_sent:

        @pl.when(cond)
        def _(copy=copy):
            copy.wait_send()

    for copy, away in z_sends:

        @pl.when(away)
        def _(copy=copy):
            copy.wait_send()

    for copy in sent:
        copy.wait_send()


def settle(a, b, c, d, a_out, b_out, c_out, d_out, a_in, b_in, c_in, d_in, sems):
    first = [
        pltpu.make_async_copy(src, dst, sems.at[n])
        for n, (src, dst) in enumerate(((a, a_in), (b, b_in), (c, c_in), (d, d_in)))
    ]
    second = [
        pltpu.make_async_copy(src, dst, sems.at[n + 4])
        for n, (src, dst) in enumerate(((a_in, a_out), (b_in, b_out), (c_in, c_out), (d_in, d_out)))
    ]
    for copy in first:
        copy.start()
    for one, two in zip(first, second):
        one.wait()
        two.start()
    for copy in second:
        copy.wait()


def on_device(patch_in, enc_weight, enc_gain, enc_bias, interp_index, queries, key_rows, value_rows, proj_weight):
    vm = pl.BlockSpec(memory_space=pltpu.VMEM)
    hbm = pl.BlockSpec(memory_space=pltpu.HBM)
    dma = pltpu.SemaphoreType.DMA
    attn, cosine, grad_attn, grad_proj = pl.pallas_call(
        kernel,
        out_shape=(
            jax.ShapeDtypeStruct((TOK, DA), BF),
            jax.ShapeDtypeStruct((1, TOK), F32),
            jax.ShapeDtypeStruct((TOK, DA), BF),
            jax.ShapeDtypeStruct((24, DA), F32),
        ),
        in_specs=[hbm] * 9,
        out_specs=(vm,) * 4,
        scratch_shapes=[
            pltpu.VMEM((192, 128), BF),
            pltpu.VMEM((192, E), BF),
            pltpu.VMEM((E,), F32),
            pltpu.VMEM((E,), F32),
            pltpu.VMEM((1, TOK), jnp.int32),
            pltpu.VMEM((E, DA), BF),
            pltpu.VMEM((NH, TOK, HD), BF),
            pltpu.VMEM((NH, TOK, HD), BF),
            pltpu.VMEM((NH, TOK, HD), BF),
            pltpu.VMEM((PH, 4, PT, HD), BF),
            pltpu.VMEM((8, TOK, HD), BF),
            pltpu.VMEM((8, TOK, HD), BF),
            pltpu.VMEM((PH, 4, PT, HD), BF),
            pltpu.VMEM((NH, TOK, HD), BF),
            pltpu.VMEM((2, 4, 16, E), F32),
            pltpu.VMEM((4, 16, E), F32),
            pltpu.VMEM((4, 16, E), BF),
            pltpu.VMEM((4, 16, E), BF),
            pltpu.VMEM((4, 4, 16, EC), BF),
            pltpu.VMEM((8, 2, 4, 16, EC), BF),
            pltpu.VMEM((TOK, EC), F32),
            pltpu.VMEM((PH, 8, SUB, EC), F32),
            pltpu.VMEM((PH, 2, 2, SUB, EC), BF),
            pltpu.VMEM((PH, 2, 2, SUB, EC), BF),
            pltpu.VMEM((PH, SUB, EC), BF),
            pltpu.VMEM((PH, SUB, EC), BF),
            pltpu.VMEM((PH, 2, SUB, EC), BF),
            pltpu.VMEM((PH, 2, SUB, EC), BF),
            pltpu.VMEM((PH, 8, SUB, EC), BF),
            pltpu.VMEM((PH, 4, 8, 128), F32),
            pltpu.VMEM((2, PH, 8, 128), F32),
            pltpu.VMEM((4, 2, BLK, DA), F32),
            pltpu.VMEM((4, BLK, DA), BF),
            pltpu.VMEM((4, BLK, DA), BF),
            pltpu.VMEM((3, BLK, DA), BF),
            pltpu.VMEM((4, BLK, DA), BF),
            pltpu.VMEM((8, 32, DA), BF),
            pltpu.VMEM((8, 32, DA), BF),
            dma((6,)),
            dma((3, NH)),
            dma((NH,)),
            dma((4,)),
            dma((4,)),
            dma((4,)),
            dma((NH,)),
            dma((4,)),
            dma((4,)),
            dma((4,)),
            dma((PH, NH)),
            dma((PH, 4)),
            dma((PH, 4)),
            dma((NH, PH)),
            dma((4,)),
            dma((4,)),
            dma((4,)),
            dma((4,)),
            dma((8,)),
            dma((8,)),
            dma((8,)),
            dma((8,)),
            dma((PH, 5)),
            dma((PH, 5)),
            dma((PH, 4)),
            dma((PH, 4)),
            dma((1,)),
            dma((1,)),
            dma((PH, 8)),
            dma((PH, 8)),
            dma((8,)),
            dma((8,)),
            dma((4, 2)),
            dma((8,)),
        ],
        compiler_params=pltpu.CompilerParams(
            collective_id=0, has_side_effects=True, vmem_limit_bytes=56 * 2**20
        ),
        name="whole",
    )(
        patch_in[0].T,
        enc_weight,
        enc_gain,
        enc_bias,
        interp_index,
        queries[0],
        key_rows[0],
        value_rows[0],
        proj_weight,
    )
    results = (attn, cosine, grad_attn, grad_proj)
    attn, cosine, grad_attn, grad_proj = pl.pallas_call(
        settle,
        out_shape=tuple(jax.ShapeDtypeStruct(a.shape, a.dtype) for a in results),
        in_specs=[hbm] * 4,
        out_specs=(hbm,) * 4,
        scratch_shapes=[pltpu.VMEM(a.shape, a.dtype) for a in results] + [dma((8,))],
        compiler_params=pltpu.CompilerParams(vmem_limit_bytes=60 * 2**20),
        name="settle",
    )(*results)
    return attn[None], cosine, grad_attn[None], grad_proj


def solution(mesh):
    placed = (
        P("dp", "head", "seq"),
        P("seq", None),
        P(),
        P(),
        P("dp", "seq"),
        P("dp", "seq", "head"),
        P("dp", "seq", "head"),
        P("dp", "seq", "head"),
        P(None, "head"),
    )
    return jax.shard_map(
        on_device,
        mesh=mesh,
        in_specs=placed,
        out_specs=(
            P("dp", "seq", "head"),
            P("dp", "seq"),
            P("dp", "seq", "head"),
            P(("dp", "seq"), "head"),
        ),
        check_vma=False,
    )
```

time: 577 us -> 110 us (0.19)
  waiting for transfers between devices: 523 us -> 0 us
  Pallas kernels: 0 us -> 109 us
  matrix products: 14.5 us -> 0 us
  between operations: 14.3 us -> 0.64 us
  local copies, waits for them, and re-layouts: 10.7 us -> 0 us
  other arithmetic: 9.87 us -> 0 us
    unnamed x7 -> x0, waiting for transfers between devices: 263 us -> none
    all_gather x3 -> x0, waiting for transfers between devices: 146 us -> none  [the longest x1 80 us: on_device(): lax.all_gather(targets, ('seq', 'head'), axis=0, tiled=True)]
    pallas_call x0 -> x2, Pallas kernels: none -> 109 us  [the longest x1 107 us: on_device(): pl.pallas_call(kernel, out_shape=(jax.ShapeDtypeStruct((TOK, DA), BF), ja...]
    psum x1 -> x0, waiting for transfers between devices: 68.5 us -> none  [on_device(): lax.psum(partial_proj.astype(jnp.bfloat16), 'head').astype(jnp.float32)]
    reduce_scatter x1 -> x0, waiting for transfers between devices: 45.2 us -> none  [on_device(): lax.psum_scatter(jnp.dot(local_patches, enc_weight, preferred_element_typ...]
    dot_general x10 -> x0, matrix products: 14.5 us -> none  [the longest x3 3.81 us: on_device(): head_outs.append(jnp.dot(probs, v_head, preferred_element_type=jnp.float32))]
    gather x1 -> x0, local copies, waits for them, and re-layouts: 5.96 us -> none  [pick_rows(): jnp.take(portion, jnp.clip(row_of_token, 0, portion.shape[0] - 1), axis=0)]
  transfers between devices with their start and end apart: 6 -> 0, of which waited for: 6 -> 0; matrix products, arithmetic and copies ran while one was open for 4% -> 0% of each run, Pallas kernels for 0% -> 0%
where the time goes in v2:
time: 110 us
  Pallas kernels  109 us (99%)
    pallas_call x1, Pallas kernels, on_device(): pl.pallas_call(kernel, out_shape=(jax.ShapeDtypeStruct((TOK, DA), BF), ja...  107 us

profile of v2, /device:TPU:1, one launch (start us, length us, event | category | flops | bytes accessed | tf_op | source)
XLA Modules:
  0.0 109.5 jit_solution(971178517428392197)
XLA Ops:
  0.6 107.1 %whole.1 = (bf16[288,384]{1,0:T(8,128)(2,1)}, f32[1,288]{1,0:T(1,128)}, bf16[288,384]{1,0:T(8,128)(2,1)}, f32[24,384]{1,0:T(8,128)}) custom-call(bf16[192,128]{1,0:T(8,128)(2,1)} %bitcast.11, bf16[192,1536]{1,0:T(8,128)(2,1)} %enc_h.1, f32[1536]{0:T(1024)} %gain_h.1, f32[1536]{0:T(1024)} %bias_h.1, s32[1,288]{1,0:T(1,128)} %idx_h.1, ...), custom_call_target="tpu_custom_call" | custom-call | tf_op jit(solution)/shard_map/whole/pallas_call | solution.py:444
  107.7 1.8 %settle.1 = (bf16[288,384]{1,0:T(8,128)(2,1)}, f32[1,288]{1,0:T(1,128)}, bf16[288,384]{1,0:T(8,128)(2,1)}, f32[24,384]{1,0:T(8,128)}) custom-call(bf16[288,384]{1,0:T(8,128)(2,1)} %get-tuple-element.12.a, f32[1,288]{1,0:T(1,128)} %get-tuple-element.13.b, bf16[288,384]{1,0:T(8,128)(2,1)} %get-tuple-element.14.c, f32[24,384]{1,0:T(8,128)} %get-tuple-element.15.d), custom_call_target="tpu_custom_call" | custom-call | tf_op jit(solution)/shard_map/settle/pallas_call | solution.py:544

commit v3 on v2

--- a/solution.py
+++ b/solution.py
@@ -18,6 +18,7 @@
 EC = 384
 PH = 3
 PT = 2 * SUB
+HB = 96
 BLK = 192
 
 layer_eps = 1e-06
@@ -39,7 +40,7 @@
     pp, s1, r1, sf, rf, s2, r2, pr, stat, cosx,
     own, g1s, g1r, g2s, g2r, g3s, g3r,
     l_s, l3_s, k_s, k_r, ks_s, ks_r, v_s, v_r, vs_s, vs_r, q_s, q_r, o_s, o_r, e_s, e_r, t_s, t_r, ty_s, ty_r, tc_s, tc_r,
-    p_s, p_r, st_s, st_r, c_s, c_r, a_s, a_r, g_s, g_r, z_s, z_r,
+    p_s, p_r, st_s, st_r, c_s, c_r, a_s, a_r, g_s, g_r, x_s, x_r, z_s, z_r,
 ):
     dp, seq, y = lax.axis_index("dp"), lax.axis_index("seq"), lax.axis_index("head")
     x, zl, zh, c = dp // 2, dp % 2, seq // 2, seq % 2
@@ -83,44 +84,6 @@
             peers.append({"dp": x * 2 + to % 2, "seq": to // 2 * 2 + cc})
     for peer in peers:
         pl.semaphore_signal(barrier, inc=1, device_id=peer, device_id_type=MESH)
-    pl.semaphore_wait(barrier, len(peers))
-
-    first = 2 * zl + 1
-    mine_r = (zh + 4 - first) % 4
-    active = mine_r < NH
-    workers = [(first + r) % 4 for r in range(NH)]
-    cond_sent = []
-
-    def go_if(cond, copy):
-        cond_sent.append((cond, copy))
-
-        @pl.when(cond)
-        def _():
-            copy.start()
-
-    def scatter(src, buf, ss, rs):
-        for r, worker in enumerate(workers):
-            go_if(worker != zh, remote(src.at[r], buf.at[seq], ss.at[r], rs.at[zh], {"seq": worker * 2 + c}))
-
-    def to_sib(buf, ss, rs, z):
-        copy = remote(buf.at[z * 2 + c], buf.at[z * 2 + c], ss.at[z], rs.at[z], at_sib)
-        copy.start()
-        return copy
-
-    def keep(src, buf, ss, rs):
-        @pl.when(active)
-        def _():
-            buf[seq] = src[mine_r]
-            to_sib(buf, ss, rs, zh)
-
-    def pass_on(buf, rs, ss2, rs2):
-        @pl.when(active)
-        def _():
-            for d in (1, 3, 2):
-                z = (zh + d) % 4
-                remote(buf.at[z * 2 + c], buf.at[z * 2 + c], rs.at[z], rs.at[z], at_sib).wait_recv()
-                to_sib(buf, ss2, rs2, z)
-
     loads[0].wait()
     loads[1].wait()
     share = lax.dot_general(
@@ -129,21 +92,98 @@
     for z in range(4):
         for cc in range(2):
             part[cc, z] = share[(2 * z + cc) * 16 : (2 * z + cc + 1) * 16]
+    for group in qkv_loads:
+        for copy in group:
+            copy.wait()
+    pl.semaphore_wait(barrier, len(peers))
+
+    first = 2 * zl + 1
+    mine_r = (zh + 4 - first) % 4
+    active = mine_r < NH
+    workers = [(first + r) % 4 for r in range(NH)]
+    cond_sent = []
+
+    def go_if(cond, copy):
+        cond_sent.append((cond, copy))
+
+        @pl.when(cond)
+        def _():
+            copy.start()
+
+    def scatter(src, buf, ss, rs):
+        for r, worker in enumerate(workers):
+            go_if(worker != zh, remote(src.at[r], buf.at[seq], ss.at[r], rs.at[zh], {"seq": worker * 2 + c}))
+
+    def to_sib(buf, ss, rs, z):
+        copy = remote(buf.at[z * 2 + c], buf.at[z * 2 + c], ss.at[z], rs.at[z], at_sib)
+        copy.start()
+        return copy
+
+    def keep(src, buf, ss, rs):
+        @pl.when(active)
+        def _():
+            buf[seq] = src[mine_r]
+            to_sib(buf, ss, rs, zh)
+
+    def pass_on(buf, rs, ss2, rs2):
+        @pl.when(active)
+        def _():
+            for d in (1, 3, 2):
+                z = (zh + d) % 4
+                remote(buf.at[z * 2 + c], buf.at[z * 2 + c], rs.at[z], rs.at[z], at_sib).wait_recv()
+                to_sib(buf, ss2, rs2, z)
+
+    scatter(k3, kb, k_s, k_r)
+    scatter(v3, vb, v_s, v_r)
+    for i in range(PH):
+        rows = slice(i * PT, (i + 1) * PT)
+        for r, worker in enumerate(workers):
+            go_if(
+                worker != zh,
+                remote(q3.at[r, rows], qb.at[i, zh], q_s.at[i, r], q_r.at[i, zh], {"seq": worker * 2 + c}),
+            )
+    keep(k3, kb, ks_s, ks_r)
+    keep(v3, vb, vs_s, vs_r)
     e1 = remote(part.at[o], e1r, e_s.at[0], e_r.at[0], at_sib)
     go(e1)
-    for copy in qkv_loads[0]:
-        copy.wait()
-    scatter(k3, kb, k_s, k_r)
-    keep(k3, kb, ks_s, ks_r)
     e1.wait_recv()
+    pass_on(kb, k_r, ks_s, ks_r)
     for d in (2, 1, 3):
         to = (zh + d) % 4
         e2s[d] = (part[c, to] + e1r[to]).astype(BF)
         go(remote(e2s.at[d], e2r.at[4 - d], e_s.at[d], e_r.at[4 - d], {"seq": to * 2 + c}))
-    for copy in qkv_loads[1]:
-        copy.wait()
-    scatter(v3, vb, v_s, v_r)
-    keep(v3, vb, vs_s, vs_r)
+    pass_on(vb, v_r, vs_s, vs_r)
+
+    @pl.when(active)
+    def _():
+        for buf, rs in ((kb, ks_r), (vb, vs_r)):
+            for z in range(4):
+                remote(buf.at[z * 2 + o], buf.at[z * 2 + o], rs.at[z], rs.at[z], at_sib).wait_recv()
+
+    def attend(i):
+        rows = slice(i * PT, (i + 1) * PT)
+        qb[i, zh] = q3[mine_r, rows]
+        for d in (1, 3, 2):
+            z = (zh + d) % 4
+            remote(qb.at[i, z], qb.at[i, z], q_r.at[i, z], q_r.at[i, z], at_sib).wait_recv()
+        scores = lax.dot_general(
+            qb[i].reshape(4 * PT, HD), kb[...].reshape(8 * TOK, HD), (((1,), (1,)), ((), ())),
+            preferred_element_type=F32,
+        )
+        top = jnp.max(scores, axis=1, keepdims=True)
+        expo = jnp.exp2((scores - top) * EXP_SCALE).astype(BF)
+        wide = jnp.concatenate([vb[...].reshape(8 * TOK, HD), jnp.ones((8 * TOK, HD), BF)], axis=1)
+        out = jnp.dot(expo, wide, preferred_element_type=F32)
+        ob[i] = (out[:, :HD] / out[:, HD:]).astype(BF).reshape(4, PT, HD)
+        for d in (2, 1, 3):
+            z = (zh + d) % 4
+            remote(ob.at[i, z], at3.at[mine_r, rows], o_s.at[i, d], o_r.at[mine_r, i], {"seq": z * 2 + c}).start()
+        at3[mine_r, rows] = ob[i, zh]
+
+    @pl.when(active)
+    def _():
+        attend(0)
+
     enc = part[c, zh] + e1r[zh]
     for d in (1, 2, 3):
         remote(e2s.at[d], e2r.at[d], e_s.at[d], e_r.at[d], at_sib).wait_recv()
@@ -161,16 +201,12 @@
     for d in (2, 1, 3):
         to = (zh + d) % 4
         go(remote(tn.at[:, zh], tn.at[:, zh], t_s.at[d], t_r.at[4 - d], {"seq": to * 2 + c}))
-    for copy in qkv_loads[2]:
-        copy.wait()
-    for i in range(PH):
-        rows = slice(i * PT, (i + 1) * PT)
-        for r, worker in enumerate(workers):
-            go_if(
-                worker != zh,
-                remote(q3.at[r, rows], qb.at[i, zh], q_s.at[i, r], q_r.at[i, zh], {"seq": worker * 2 + c}),
-            )
-    pass_on(kb, k_r, ks_s, ks_r)
+
+    @pl.when(active)
+    def _():
+        attend(1)
+        attend(2)
+
     for d in (1, 2, 3):
         fr = (zh + d) % 4
         remote(tn.at[:, fr], tn.at[:, fr], t_s.at[d], t_r.at[d], at_sib).wait_recv()
@@ -195,33 +231,6 @@
         go(remote(at(far), at(far), ss(6), rs(4), at_y(2 + 4 * odd)))
         go(remote(at(lo), at(lo), ss(4), rs(5), at_y(1)))
         go(remote(at(hi), at(hi), ss(5), rs(3), at_y(7)))
-
-    pass_on(vb, v_r, vs_s, vs_r)
-
-    @pl.when(active)
-    def _():
-        for buf, rs in ((kb, ks_r), (vb, vs_r)):
-            for z in range(4):
-                remote(buf.at[z * 2 + o], buf.at[z * 2 + o], rs.at[z], rs.at[z], at_sib).wait_recv()
-        for i in range(PH):
-            rows = slice(i * PT, (i + 1) * PT)
-            qb[i, zh] = q3[mine_r, rows]
-            for d in (1, 3, 2):
-                z = (zh + d) % 4
-                remote(qb.at[i, z], qb.at[i, z], q_r.at[i, z], q_r.at[i, z], at_sib).wait_recv()
-            scores = lax.dot_general(
-                qb[i].reshape(4 * PT, HD), kb[...].reshape(8 * TOK, HD), (((1,), (1,)), ((), ())),
-                preferred_element_type=F32,
-            )
-            top = jnp.max(scores, axis=1, keepdims=True)
-            expo = jnp.exp2((scores - top) * EXP_SCALE).astype(BF)
-            wide = jnp.concatenate([vb[...].reshape(8 * TOK, HD), jnp.ones((8 * TOK, HD), BF)], axis=1)
-            out = jnp.dot(expo, wide, preferred_element_type=F32)
-            ob[i] = (out[:, :HD] / out[:, HD:]).astype(BF).reshape(4, PT, HD)
-            for d in (2, 1, 3):
-                z = (zh + d) % 4
-                remote(ob.at[i, z], at3.at[mine_r, rows], o_s.at[i, d], o_r.at[mine_r, i], {"seq": z * 2 + c}).start()
-            at3[mine_r, rows] = ob[i, zh]
 
     loads[5].wait()
 
@@ -340,33 +349,32 @@
     for n, (xx, d) in enumerate(((xo, 2), (xu, 1), (xd, 3))):
         remote(g1s.at[n], g1r.at[n], g_s.at[n], g_r.at[n], at_sib).wait_recv()
         g2s[n] = (own[xx, c] + g1r[n].astype(F32)).astype(BF)
-        go(remote(g2s.at[n], g2r.at[4 - d], g_s.at[3 + d], g_r.at[8 - d], {"dp": xx * 2 + zl}))
+        first_rows = slice(0, HB)
+        go(remote(g2s.at[n, first_rows], g2r.at[4 - d, first_rows], x_s.at[0, d], x_r.at[0, 4 - d], {"dp": xx * 2 + zl}))
+    for n, (xx, d) in enumerate(((xo, 2), (xu, 1), (xd, 3))):
+        last_rows = slice(HB, BLK)
+        go(remote(g2s.at[n, last_rows], g2r.at[4 - d, last_rows], x_s.at[1, d], x_r.at[1, 4 - d], {"dp": xx * 2 + zl}))
     back = jnp.dot(grad_columns(0), w[:EC], preferred_element_type=F32)
     for e in range(1, 4):
         back = back + jnp.dot(grad_columns(e), w[e * EC : (e + 1) * EC], preferred_element_type=F32)
     grad_attn[...] = back.astype(BF)
     remote(g1s.at[3], g1r.at[3], g_s.at[3], g_r.at[3], at_sib).wait_recv()
-    mine = own[x, c] + g1r[3].astype(F32)
-    for d in (1, 3, 2):
-        remote(g2s.at[0], g2r.at[d], g_s.at[3 + d], g_r.at[4 + d], {"dp": xu * 2 + zl}).wait_recv()
-        mine = mine + g2r[d].astype(F32)
-    for n in range(8):
-        g3s[n] = jnp.concatenate([mine[n * 24 : (n + 1) * 24], jnp.zeros((8, DA), F32)], axis=0).astype(BF)
-    z_sends = []
-    for dz in range(4):
-        for cc in range(2):
-            to = (zh + dz) % 4
-            copy = remote(g3s.at[to * 2 + cc], g3r.at[pos], z_s.at[dz, cc], z_r.at[pos],
-                          {"dp": x * 2 + c, "seq": to * 2 + cc})
-            if dz == 0:
-                away = (zl != c) | (c != cc)
-                z_sends.append((copy, away))
-
-                @pl.when(away)
-                def _(copy=copy):
-                    copy.start()
-            else:
-                go(copy)
+    for part_of in range(2):
+        rows = slice(part_of * HB, (part_of + 1) * HB)
+        mine = own[x, c, rows] + g1r[3, rows].astype(F32)
+        for d in (1, 3, 2):
+            remote(g2s.at[0, rows], g2r.at[d, rows], x_s.at[part_of, d], x_r.at[part_of, d], at_sib).wait_recv()
+            mine = mine + g2r[d, rows].astype(F32)
+        for n in range(4):
+            piece = jnp.concatenate([mine[n * 24 : (n + 1) * 24], jnp.zeros((8, DA), F32)], axis=0)
+            g3s[part_of * 4 + n] = piece.astype(BF)
+        for n in range(4):
+            tz, cc = part_of * 2 + n // 2, n % 2
+            go_if(
+                (tz != zh) | (zl != c) | (c != cc),
+                remote(g3s.at[tz * 2 + cc], g3r.at[pos], z_s.at[tz, cc], z_r.at[pos],
+                       {"dp": x * 2 + c, "seq": tz * 2 + cc}),
+            )
     row = jnp.zeros((8, 384), F32)
     token = lax.broadcasted_iota(jnp.int32, (8, 384), 1)
     remote(cosx.at[0], cosx.at[1], c_s.at[0], c_r.at[0], at_y(4)).wait_recv()
@@ -406,12 +414,6 @@
     for cond, copy in cond_sent:
 
         @pl.when(cond)
-        def _(copy=copy):
-            copy.wait_send()
-
-    for copy, away in z_sends:
-
-        @pl.when(away)
         def _(copy=copy):
             copy.wait_send()
 
@@ -520,8 +522,10 @@
             dma((1,)),
             dma((PH, 8)),
             dma((PH, 8)),
-            dma((8,)),
-            dma((8,)),
+            dma((4,)),
+            dma((4,)),
+            dma((2, 4)),
+            dma((2, 4)),
             dma((4, 2)),
             dma((8,)),
         ],

time: 110 us -> 110 us (level)
  no operation moved by 1% of the time
where the time goes in v3:
time: 110 us
  Pallas kernels  109 us (99%)
    pallas_call x1, Pallas kernels, on_device(): pl.pallas_call(kernel, out_shape=(jax.ShapeDtypeStruct((TOK, DA), BF), ja...  107 us

profile of v3, /device:TPU:1, one launch (start us, length us, event | category | flops | bytes accessed | tf_op | source)
XLA Modules:
  0.0 109.9 jit_solution(1697851182977025270)
XLA Ops:
  0.6 107.4 %whole.1 = (bf16[288,384]{1,0:T(8,128)(2,1)}, f32[1,288]{1,0:T(1,128)}, bf16[288,384]{1,0:T(8,128)(2,1)}, f32[24,384]{1,0:T(8,128)}) custom-call(bf16[192,128]{1,0:T(8,128)(2,1)} %bitcast.11, bf16[192,1536]{1,0:T(8,128)(2,1)} %enc_h.1, f32[1536]{0:T(1024)} %gain_h.1, f32[1536]{0:T(1024)} %bias_h.1, s32[1,288]{1,0:T(1,128)} %idx_h.1, ...), custom_call_target="tpu_custom_call" | custom-call | tf_op jit(solution)/shard_map/whole/pallas_call | solution.py:446
  108.1 1.8 %settle.1 = (bf16[288,384]{1,0:T(8,128)(2,1)}, f32[1,288]{1,0:T(1,128)}, bf16[288,384]{1,0:T(8,128)(2,1)}, f32[24,384]{1,0:T(8,128)}) custom-call(bf16[288,384]{1,0:T(8,128)(2,1)} %get-tuple-element.12.a, f32[1,288]{1,0:T(1,128)} %get-tuple-element.13.b, bf16[288,384]{1,0:T(8,128)(2,1)} %get-tuple-element.14.c, f32[24,384]{1,0:T(8,128)} %get-tuple-element.15.d), custom_call_target="tpu_custom_call" | custom-call | tf_op jit(solution)/shard_map/settle/pallas_call | solution.py:548

commit v4 on v3

--- a/solution.py
+++ b/solution.py
@@ -207,13 +207,6 @@
         attend(1)
         attend(2)
 
-    for d in (1, 2, 3):
-        fr = (zh + d) % 4
-        remote(tn.at[:, fr], tn.at[:, fr], t_s.at[d], t_r.at[d], at_sib).wait_recv()
-    for d in (4, 3, 5, 2, 6, 1, 7):
-        go(remote(tn.at[(y + d) % 4], tb.at[y, c], ty_s.at[d], ty_r.at[8 - d], at_y(d)))
-    tb[y, c] = tn[chunk]
-
     def gather_start(at, ss, rs):
         for n, d in enumerate((2, 6, 1, 7)):
             go(remote(at(y), at(y), ss(n), rs(8 - d), at_y(d)))
@@ -257,11 +250,13 @@
         s1[i, 1, 1] = pp[i, (y + 5) % 8].astype(BF)
         s1[i, 1, 0] = pp[i, (y + 7) % 8].astype(BF)
         go(remote(s1.at[i, 1], r1.at[i, 1], p_s.at[i, 2], p_r.at[i, 2], at_y(7)))
-    for d in range(1, 8):
-        fr = (y + d) % 8
-        remote(tb.at[fr, c], tb.at[fr, c], ty_s.at[d], ty_r.at[d], at_y(d)).wait_recv()
-    to_core = remote(tb.at[:, c], tb.at[:, c], tc_s.at[0], tc_r.at[0], at_sib)
-    go(to_core)
+    for d in (1, 2, 3):
+        fr = (zh + d) % 4
+        remote(tn.at[:, fr], tn.at[:, fr], t_s.at[d], t_r.at[d], at_sib).wait_recv()
+    for d in (4, 3, 5, 2, 6, 1, 7):
+        go(remote(tn.at[(y + d) % 4], tb.at[y, c], ty_s.at[d], ty_r.at[8 - d], at_y(d)))
+    tb[y, c] = tn[chunk]
+
     for i in range(PH):
         remote(sf.at[i], rf.at[i], p_s.at[i, 0], p_r.at[i, 0], at_y(1)).wait_recv()
         remote(s1.at[i, 0], r1.at[i, 0], p_s.at[i, 1], p_r.at[i, 1], at_y(1)).wait_recv()
@@ -274,6 +269,11 @@
         s2[i, 1] = jnp.where(odd == 1, lower + far, lower).astype(BF)
         go(remote(s2.at[i, 1], r2.at[i, 1], p_s.at[i, 4], p_r.at[i, 4], at_y(6)))
 
+    for d in range(1, 8):
+        fr = (y + d) % 8
+        remote(tb.at[fr, c], tb.at[fr, c], ty_s.at[d], ty_r.at[d], at_y(d)).wait_recv()
+    to_core = remote(tb.at[:, c], tb.at[:, c], tc_s.at[0], tc_r.at[0], at_sib)
+    go(to_core)
     loads[4].wait()
     picks = idx[...]
     rest = picks % 128

time: 110 us -> 111 us (level)
  no operation moved by 1% of the time
where the time goes in v4:
time: 111 us
  Pallas kernels  110 us (99%)
    pallas_call x1, Pallas kernels, on_device(): pl.pallas_call(kernel, out_shape=(jax.ShapeDtypeStruct((TOK, DA), BF), ja...  108 us

profile of v4, /device:TPU:1, one launch (start us, length us, event | category | flops | bytes accessed | tf_op | source)
XLA Modules:
  0.0 110.7 jit_solution(15727852656931675027)
XLA Ops:
  0.6 108.3 %whole.1 = (bf16[288,384]{1,0:T(8,128)(2,1)}, f32[1,288]{1,0:T(1,128)}, bf16[288,384]{1,0:T(8,128)(2,1)}, f32[24,384]{1,0:T(8,128)}) custom-call(bf16[192,128]{1,0:T(8,128)(2,1)} %bitcast.11, bf16[192,1536]{1,0:T(8,128)(2,1)} %enc_h.1, f32[1536]{0:T(1024)} %gain_h.1, f32[1536]{0:T(1024)} %bias_h.1, s32[1,288]{1,0:T(1,128)} %idx_h.1, ...), custom_call_target="tpu_custom_call" | custom-call | tf_op jit(solution)/shard_map/whole/pallas_call | solution.py:446
  108.9 1.8 %settle.1 = (bf16[288,384]{1,0:T(8,128)(2,1)}, f32[1,288]{1,0:T(1,128)}, bf16[288,384]{1,0:T(8,128)(2,1)}, f32[24,384]{1,0:T(8,128)}) custom-call(bf16[288,384]{1,0:T(8,128)(2,1)} %get-tuple-element.12.a, f32[1,288]{1,0:T(1,128)} %get-tuple-element.13.b, bf16[288,384]{1,0:T(8,128)(2,1)} %get-tuple-element.14.c, f32[24,384]{1,0:T(8,128)} %get-tuple-element.15.d), custom_call_target="tpu_custom_call" | custom-call | tf_op jit(solution)/shard_map/settle/pallas_call | solution.py:548

commit v5 on v4

--- a/solution.py
+++ b/solution.py
@@ -134,7 +134,35 @@
                 to_sib(buf, ss2, rs2, z)
 
     scatter(k3, kb, k_s, k_r)
+    keep(k3, kb, ks_s, ks_r)
+    e1 = remote(part.at[o], e1r, e_s.at[0], e_r.at[0], at_sib)
+    go(e1)
+    e1.wait_recv()
+    for d in (2, 1, 3):
+        to = (zh + d) % 4
+        e2s[d] = (part[c, to] + e1r[to]).astype(BF)
+        go(remote(e2s.at[d], e2r.at[4 - d], e_s.at[d], e_r.at[4 - d], {"seq": to * 2 + c}))
     scatter(v3, vb, v_s, v_r)
+    keep(v3, vb, vs_s, vs_r)
+    pass_on(kb, k_r, ks_s, ks_r)
+    enc = part[c, zh] + e1r[zh]
+    for d in (1, 2, 3):
+        remote(e2s.at[d], e2r.at[d], e_s.at[d], e_r.at[d], at_sib).wait_recv()
+        enc = enc + e2r[d].astype(F32)
+    loads[2].wait()
+    loads[3].wait()
+    average = jnp.mean(enc, axis=1, keepdims=True)
+    centred = enc - average
+    variance = jnp.mean(centred * centred, axis=1, keepdims=True)
+    normed = (
+        centred * lax.rsqrt(variance + layer_eps) * gain[...].reshape(1, E) + bias[...].reshape(1, E)
+    ).astype(BF)
+    for e in range(4):
+        tn[e, zh] = normed[:, e * EC : (e + 1) * EC]
+    for d in (2, 1, 3):
+        to = (zh + d) % 4
+        go(remote(tn.at[:, zh], tn.at[:, zh], t_s.at[d], t_r.at[4 - d], {"seq": to * 2 + c}))
+
     for i in range(PH):
         rows = slice(i * PT, (i + 1) * PT)
         for r, worker in enumerate(workers):
@@ -142,17 +170,13 @@
                 worker != zh,
                 remote(q3.at[r, rows], qb.at[i, zh], q_s.at[i, r], q_r.at[i, zh], {"seq": worker * 2 + c}),
             )
-    keep(k3, kb, ks_s, ks_r)
-    keep(v3, vb, vs_s, vs_r)
-    e1 = remote(part.at[o], e1r, e_s.at[0], e_r.at[0], at_sib)
-    go(e1)
-    e1.wait_recv()
-    pass_on(kb, k_r, ks_s, ks_r)
-    for d in (2, 1, 3):
-        to = (zh + d) % 4
-        e2s[d] = (part[c, to] + e1r[to]).astype(BF)
-        go(remote(e2s.at[d], e2r.at[4 - d], e_s.at[d], e_r.at[4 - d], {"seq": to * 2 + c}))
     pass_on(vb, v_r, vs_s, vs_r)
+    for d in (1, 2, 3):
+        fr = (zh + d) % 4
+        remote(tn.at[:, fr], tn.at[:, fr], t_s.at[d], t_r.at[d], at_sib).wait_recv()
+    for d in (4, 3, 5, 2, 6, 1, 7):
+        go(remote(tn.at[(y + d) % 4], tb.at[y, c], ty_s.at[d], ty_r.at[8 - d], at_y(d)))
+    tb[y, c] = tn[chunk]
 
     @pl.when(active)
     def _():
@@ -183,27 +207,6 @@
     @pl.when(active)
     def _():
         attend(0)
-
-    enc = part[c, zh] + e1r[zh]
-    for d in (1, 2, 3):
-        remote(e2s.at[d], e2r.at[d], e_s.at[d], e_r.at[d], at_sib).wait_recv()
-        enc = enc + e2r[d].astype(F32)
-    loads[2].wait()
-    loads[3].wait()
-    average = jnp.mean(enc, axis=1, keepdims=True)
-    centred = enc - average
-    variance = jnp.mean(centred * centred, axis=1, keepdims=True)
-    normed = (
-        centred * lax.rsqrt(variance + layer_eps) * gain[...].reshape(1, E) + bias[...].reshape(1, E)
-    ).astype(BF)
-    for e in range(4):
-        tn[e, zh] = normed[:, e * EC : (e + 1) * EC]
-    for d in (2, 1, 3):
-        to = (zh + d) % 4
-        go(remote(tn.at[:, zh], tn.at[:, zh], t_s.at[d], t_r.at[4 - d], {"seq": to * 2 + c}))
-
-    @pl.when(active)
-    def _():
         attend(1)
         attend(2)
 
@@ -250,13 +253,6 @@
         s1[i, 1, 1] = pp[i, (y + 5) % 8].astype(BF)
         s1[i, 1, 0] = pp[i, (y + 7) % 8].astype(BF)
         go(remote(s1.at[i, 1], r1.at[i, 1], p_s.at[i, 2], p_r.at[i, 2], at_y(7)))
-    for d in (1, 2, 3):
-        fr = (zh + d) % 4
-        remote(tn.at[:, fr], tn.at[:, fr], t_s.at[d], t_r.at[d], at_sib).wait_recv()
-    for d in (4, 3, 5, 2, 6, 1, 7):
-        go(remote(tn.at[(y + d) % 4], tb.at[y, c], ty_s.at[d], ty_r.at[8 - d], at_y(d)))
-    tb[y, c] = tn[chunk]
-
     for i in range(PH):
         remote(sf.at[i], rf.at[i], p_s.at[i, 0], p_r.at[i, 0], at_y(1)).wait_recv()
         remote(s1.at[i, 0], r1.at[i, 0], p_s.at[i, 1], p_r.at[i, 1], at_y(1)).wait_recv()

time: 111 us -> 106 us (0.955)
  Pallas kernels: 110 us -> 105 us
    pallas_call x1, Pallas kernels: 108 us -> 103 us  [on_device(): pl.pallas_call(kernel, out_shape=(jax.ShapeDtypeStruct((TOK, DA), BF), ja...]
where the time goes in v5:
time: 106 us
  Pallas kernels  105 us (99%)
    pallas_call x1, Pallas kernels, on_device(): pl.pallas_call(kernel, out_shape=(jax.ShapeDtypeStruct((TOK, DA), BF), ja...  103 us

profile of v5, /device:TPU:1, one launch (start us, length us, event | category | flops | bytes accessed | tf_op | source)
XLA Modules:
  0.0 105.8 jit_solution(2217960069624002837)
XLA Ops:
  0.6 103.3 %whole.1 = (bf16[288,384]{1,0:T(8,128)(2,1)}, f32[1,288]{1,0:T(1,128)}, bf16[288,384]{1,0:T(8,128)(2,1)}, f32[24,384]{1,0:T(8,128)}) custom-call(bf16[192,128]{1,0:T(8,128)(2,1)} %bitcast.11, bf16[192,1536]{1,0:T(8,128)(2,1)} %enc_h.1, f32[1536]{0:T(1024)} %gain_h.1, f32[1536]{0:T(1024)} %bias_h.1, s32[1,288]{1,0:T(1,128)} %idx_h.1, ...), custom_call_target="tpu_custom_call" | custom-call | tf_op jit(solution)/shard_map/whole/pallas_call | solution.py:442
  104.0 1.8 %settle.1 = (bf16[288,384]{1,0:T(8,128)(2,1)}, f32[1,288]{1,0:T(1,128)}, bf16[288,384]{1,0:T(8,128)(2,1)}, f32[24,384]{1,0:T(8,128)}) custom-call(bf16[288,384]{1,0:T(8,128)(2,1)} %get-tuple-element.12.a, f32[1,288]{1,0:T(1,128)} %get-tuple-element.13.b, bf16[288,384]{1,0:T(8,128)(2,1)} %get-tuple-element.14.c, f32[24,384]{1,0:T(8,128)} %get-tuple-element.15.d), custom_call_target="tpu_custom_call" | custom-call | tf_op jit(solution)/shard_map/settle/pallas_call | solution.py:544

commit v6 on v5

--- a/solution.py
+++ b/solution.py
@@ -18,7 +18,7 @@
 EC = 384
 PH = 3
 PT = 2 * SUB
-HB = 96
+HB = 48
 BLK = 192
 
 layer_eps = 1e-06
@@ -97,7 +97,7 @@
             copy.wait()
     pl.semaphore_wait(barrier, len(peers))
 
-    first = 2 * zl + 1
+    first = zl + 1
     mine_r = (zh + 4 - first) % 4
     active = mine_r < NH
     workers = [(first + r) % 4 for r in range(NH)]
@@ -345,27 +345,31 @@
     for n, (xx, d) in enumerate(((xo, 2), (xu, 1), (xd, 3))):
         remote(g1s.at[n], g1r.at[n], g_s.at[n], g_r.at[n], at_sib).wait_recv()
         g2s[n] = (own[xx, c] + g1r[n].astype(F32)).astype(BF)
-        first_rows = slice(0, HB)
-        go(remote(g2s.at[n, first_rows], g2r.at[4 - d, first_rows], x_s.at[0, d], x_r.at[0, 4 - d], {"dp": xx * 2 + zl}))
-    for n, (xx, d) in enumerate(((xo, 2), (xu, 1), (xd, 3))):
-        last_rows = slice(HB, BLK)
-        go(remote(g2s.at[n, last_rows], g2r.at[4 - d, last_rows], x_s.at[1, d], x_r.at[1, 4 - d], {"dp": xx * 2 + zl}))
+        rows = slice(0, HB)
+        go(remote(g2s.at[n, rows], g2r.at[4 - d, rows], x_s.at[0, d], x_r.at[0, 4 - d], {"dp": xx * 2 + zl}))
+    for part_of in range(1, 4):
+        for n, (xx, d) in enumerate(((xo, 2), (xu, 1), (xd, 3))):
+            rows = slice(part_of * HB, (part_of + 1) * HB)
+            go(
+                remote(g2s.at[n, rows], g2r.at[4 - d, rows], x_s.at[part_of, d], x_r.at[part_of, 4 - d],
+                       {"dp": xx * 2 + zl})
+            )
     back = jnp.dot(grad_columns(0), w[:EC], preferred_element_type=F32)
     for e in range(1, 4):
         back = back + jnp.dot(grad_columns(e), w[e * EC : (e + 1) * EC], preferred_element_type=F32)
     grad_attn[...] = back.astype(BF)
     remote(g1s.at[3], g1r.at[3], g_s.at[3], g_r.at[3], at_sib).wait_recv()
-    for part_of in range(2):
+    for part_of in range(4):
         rows = slice(part_of * HB, (part_of + 1) * HB)
         mine = own[x, c, rows] + g1r[3, rows].astype(F32)
         for d in (1, 3, 2):
             remote(g2s.at[0, rows], g2r.at[d, rows], x_s.at[part_of, d], x_r.at[part_of, d], at_sib).wait_recv()
             mine = mine + g2r[d, rows].astype(F32)
-        for n in range(4):
+        for n in range(2):
             piece = jnp.concatenate([mine[n * 24 : (n + 1) * 24], jnp.zeros((8, DA), F32)], axis=0)
-            g3s[part_of * 4 + n] = piece.astype(BF)
-        for n in range(4):
-            tz, cc = part_of * 2 + n // 2, n % 2
+            g3s[part_of * 2 + n] = piece.astype(BF)
+        for n in range(2):
+            tz, cc = part_of, n
             go_if(
                 (tz != zh) | (zl != c) | (c != cc),
                 remote(g3s.at[tz * 2 + cc], g3r.at[pos], z_s.at[tz, cc], z_r.at[pos],
@@ -520,8 +524,8 @@
             dma((PH, 8)),
             dma((4,)),
             dma((4,)),
-            dma((2, 4)),
-            dma((2, 4)),
+            dma((4, 4)),
+            dma((4, 4)),
             dma((4, 2)),
             dma((8,)),
         ],

time: 106 us -> 102 us (0.962)
  Pallas kernels: 105 us -> 101 us
    pallas_call x1, Pallas kernels: 103 us -> 99.4 us  [on_device(): pl.pallas_call(kernel, out_shape=(jax.ShapeDtypeStruct((TOK, DA), BF), ja...]
where the time goes in v6:
time: 102 us
  Pallas kernels  101 us (99%)
    pallas_call x1, Pallas kernels, on_device(): pl.pallas_call(kernel, out_shape=(jax.ShapeDtypeStruct((TOK, DA), BF), ja...  99.4 us

profile of v6, /device:TPU:1, one launch (start us, length us, event | category | flops | bytes accessed | tf_op | source)
XLA Modules:
  0.0 101.9 jit_solution(3820336947430575920)
XLA Ops:
  0.6 99.4 %whole.1 = (bf16[288,384]{1,0:T(8,128)(2,1)}, f32[1,288]{1,0:T(1,128)}, bf16[288,384]{1,0:T(8,128)(2,1)}, f32[24,384]{1,0:T(8,128)}) custom-call(bf16[192,128]{1,0:T(8,128)(2,1)} %bitcast.11, bf16[192,1536]{1,0:T(8,128)(2,1)} %enc_h.1, f32[1536]{0:T(1024)} %gain_h.1, f32[1536]{0:T(1024)} %bias_h.1, s32[1,288]{1,0:T(1,128)} %idx_h.1, ...), custom_call_target="tpu_custom_call" | custom-call | tf_op jit(solution)/shard_map/whole/pallas_call | solution.py:446
  100.1 1.8 %settle.1 = (bf16[288,384]{1,0:T(8,128)(2,1)}, f32[1,288]{1,0:T(1,128)}, bf16[288,384]{1,0:T(8,128)(2,1)}, f32[24,384]{1,0:T(8,128)}) custom-call(bf16[288,384]{1,0:T(8,128)(2,1)} %get-tuple-element.12.a, f32[1,288]{1,0:T(1,128)} %get-tuple-element.13.b, bf16[288,384]{1,0:T(8,128)(2,1)} %get-tuple-element.14.c, f32[24,384]{1,0:T(8,128)} %get-tuple-element.15.d), custom_call_target="tpu_custom_call" | custom-call | tf_op jit(solution)/shard_map/settle/pallas_call | solution.py:548

commit v7 on v6

--- a/solution.py
+++ b/solution.py
@@ -134,6 +134,7 @@
                 to_sib(buf, ss2, rs2, z)
 
     scatter(k3, kb, k_s, k_r)
+    scatter(v3, vb, v_s, v_r)
     keep(k3, kb, ks_s, ks_r)
     e1 = remote(part.at[o], e1r, e_s.at[0], e_r.at[0], at_sib)
     go(e1)
@@ -142,7 +143,6 @@
         to = (zh + d) % 4
         e2s[d] = (part[c, to] + e1r[to]).astype(BF)
         go(remote(e2s.at[d], e2r.at[4 - d], e_s.at[d], e_r.at[4 - d], {"seq": to * 2 + c}))
-    scatter(v3, vb, v_s, v_r)
     keep(v3, vb, vs_s, vs_r)
     pass_on(kb, k_r, ks_s, ks_r)
     enc = part[c, zh] + e1r[zh]

time: 102 us -> 102 us (level)
  no operation moved by 1% of the time
where the time goes in v7:
time: 102 us; the launch traced here: 101 us
  Pallas kernels  101 us (99%)
    pallas_call x1, Pallas kernels, on_device(): pl.pallas_call(kernel, out_shape=(jax.ShapeDtypeStruct((TOK, DA), BF), ja...  99 us

profile of v7, /device:TPU:1, one launch (start us, length us, event | category | flops | bytes accessed | tf_op | source)
XLA Modules:
  0.0 101.5 jit_solution(5539946035221511696)
XLA Ops:
  0.6 99.0 %whole.1 = (bf16[288,384]{1,0:T(8,128)(2,1)}, f32[1,288]{1,0:T(1,128)}, bf16[288,384]{1,0:T(8,128)(2,1)}, f32[24,384]{1,0:T(8,128)}) custom-call(bf16[192,128]{1,0:T(8,128)(2,1)} %bitcast.11, bf16[192,1536]{1,0:T(8,128)(2,1)} %enc_h.1, f32[1536]{0:T(1024)} %gain_h.1, f32[1536]{0:T(1024)} %bias_h.1, s32[1,288]{1,0:T(1,128)} %idx_h.1, ...), custom_call_target="tpu_custom_call" | custom-call | tf_op jit(solution)/shard_map/whole/pallas_call | solution.py:446
  99.6 1.8 %settle.1 = (bf16[288,384]{1,0:T(8,128)(2,1)}, f32[1,288]{1,0:T(1,128)}, bf16[288,384]{1,0:T(8,128)(2,1)}, f32[24,384]{1,0:T(8,128)}) custom-call(bf16[288,384]{1,0:T(8,128)(2,1)} %get-tuple-element.12.a, f32[1,288]{1,0:T(1,128)} %get-tuple-element.13.b, bf16[288,384]{1,0:T(8,128)(2,1)} %get-tuple-element.14.c, f32[24,384]{1,0:T(8,128)} %get-tuple-element.15.d), custom_call_target="tpu_custom_call" | custom-call | tf_op jit(solution)/shard_map/settle/pallas_call | solution.py:548
